TPU v7x, 256 devices: a whole 4x4x8 slice. The times are simulated.
256 devices in a mesh: context: 32 (over z, x), tensor: 8 (over y, core).
Axes of the slice: x: 4, y: 4, z: 8, core: 2. Of those that a mesh axis runs over, the one named last changes fastest.
Arguments:
- tokens: bfloat16 [4096, 8192], P('context', 'tensor'), may hold values from -40 to 40
- norm_gain: float32 [8192], P('tensor'), may hold values from 0.1 to 1.9
- router: bfloat16 [8192], P('tensor'), may hold values from -0.0625 to 0.0625
- w_gate: bfloat16 [8192, 28672], P('tensor', 'context'), may hold values from -0.0625 to 0.0625
- w_up: bfloat16 [8192, 28672], P('tensor', 'context'), may hold values from -0.0625 to 0.0625
- w_down: bfloat16 [28672, 8192], P('context', 'tensor'), may hold values from -0.03125 to 0.03125
- routes: int32 [32, 24], P('context'), may hold values from 0 to 127, as said below
- counts: int32 [32], P('context'), may hold values from 1 to 24, 512 in all
- cotangent: bfloat16 [4096, 8192], P('context', 'tensor'), may hold values from -6 to 6
Outputs:
- mixed: bfloat16 [4096, 8192], P('context', 'tensor')
- grad_tokens: bfloat16 [4096, 8192], P('context', 'tensor')
- grad_gate: bfloat16 [8192, 28672], P('tensor', 'context')
- grad_up: bfloat16 [8192, 28672], P('tensor', 'context')
- grad_down: bfloat16 [28672, 8192], P('context', 'tensor')
- grad_gain: float32 [8192], P('tensor')
- grad_router: float32 [8192], P('tensor')
Inputs may be any that keep to these rules, and one draw needn't show every extreme that they name: `routes`: within a row the 24 entries are distinct local positions; only the first counts entries of a row are used. The counts add up to 512; the largest is 24.
All inputs are finite; a program needn't handle non-finite values. No bound on the sum of `counts` on one device may be relied on, other than what follows from the above.
Results may differ from a plain program's by a relative error of at most 0.015.
Values may be sent and summed in bfloat16 or wider, within the bound.
A program may use at most 64 MiB of HBM per device.

v0:
```python
import jax
import jax.numpy as jnp
from jax import lax
from jax.sharding import PartitionSpec as P

D = 8192


EPS = 1e-05


def contract_rows(left, right):
    return lax.dot_general(
        left, right, (((0,), (0,)), ((), ())), preferred_element_type=jnp.float32
    )


def contract_cols(left, right):
    return lax.dot_general(
        left, right, (((1,), (1,)), ((), ())), preferred_element_type=jnp.float32
    )


def body(tokens, norm_gain, router, w_gate, w_up, w_down, routes, counts, cotangent):
    capacity = routes.shape[1]
    inner = w_gate.shape[1]
    live_count = counts[0]
    slot_ids = jnp.arange(capacity, dtype=jnp.int32)
    usable = (slot_ids < live_count)[:, None]
    local_ids = routes[0]
    picked_low = jnp.take(tokens, local_ids, axis=0)
    picked = picked_low.astype(jnp.float32)
    squares, logit = lax.psum(
        (
            jnp.sum(picked * picked, axis=1),
            jnp.dot(picked_low, router, preferred_element_type=jnp.float32),
        ),
        "tensor",
    )
    inv_rms = lax.rsqrt(squares / D + EPS)[:, None]
    scaled = picked * inv_rms
    normed = jnp.where(usable, scaled * norm_gain, 0.0).astype(jnp.bfloat16)
    weight = jax.nn.sigmoid(logit)[:, None]
    normed_pad = lax.all_gather(normed, "context", axis=0, tiled=True)
    gate_upward = lax.psum_scatter(
        jnp.concatenate(
            [
                jnp.dot(normed_pad, w_gate, preferred_element_type=jnp.float32),
                jnp.dot(normed_pad, w_up, preferred_element_type=jnp.float32),
            ],
            axis=1,
        ),
        "tensor",
        scatter_dimension=0,
        tiled=True,
    )
    gate = gate_upward[:, :inner]
    upward = gate_upward[:, inner:]
    hidden = (jax.nn.silu(gate) * upward).astype(jnp.bfloat16)
    hidden_all = lax.all_gather(hidden, "tensor", axis=0, tiled=True)
    branch = lax.psum_scatter(
        jnp.dot(hidden_all, w_down, preferred_element_type=jnp.float32).astype(jnp.bfloat16),
        "context",
        scatter_dimension=0,
        tiled=True,
    ).astype(jnp.float32)
    mixed_rows = (picked + weight * branch).astype(jnp.bfloat16)
    mixed = tokens.at[local_ids].set(jnp.where(usable, mixed_rows, picked_low))
    slope = jnp.take(cotangent, local_ids, axis=0).astype(jnp.float32)
    d_branch = jnp.where(usable, weight * slope, 0.0).astype(jnp.bfloat16)
    d_branch_pad = lax.all_gather(d_branch, "context", axis=0, tiled=True)
    branch_inner = lax.psum(jnp.sum(slope * branch, axis=1), "tensor")
    d_logit = jnp.where(usable, branch_inner[:, None] * weight * (1.0 - weight), 0.0)
    d_hidden = lax.psum_scatter(
        contract_cols(d_branch_pad, w_down), "tensor", scatter_dimension=0, tiled=True
    )
    sigma = jax.nn.sigmoid(gate)
    d_gate = (d_hidden * upward * sigma * (1.0 + gate * (1.0 - sigma))).astype(jnp.bfloat16)
    d_upward = (d_hidden * gate * sigma).astype(jnp.bfloat16)
    grad_down = contract_rows(hidden_all, d_branch_pad).astype(jnp.bfloat16)
    d_gate_all, d_upward_all = (
        lax.all_gather(d_gate, "tensor", axis=0, tiled=True),
        lax.all_gather(d_upward, "tensor", axis=0, tiled=True),
    )
    grad_gate = contract_rows(normed_pad, d_gate_all).astype(jnp.bfloat16)
    grad_up = contract_rows(normed_pad, d_upward_all).astype(jnp.bfloat16)
    d_normed = lax.psum_scatter(
        (contract_cols(d_gate_all, w_gate) + contract_cols(d_upward_all, w_up)).astype(
            jnp.bfloat16
        ),
        "context",
        scatter_dimension=0,
        tiled=True,
    ).astype(jnp.float32)
    d_scaled = d_normed * norm_gain
    mean_term = lax.psum(jnp.sum(d_scaled * picked, axis=1), "tensor")[:, None] / D
    d_picked = inv_rms * (
        d_scaled - picked * inv_rms * inv_rms * mean_term
    ) + d_logit * router.astype(jnp.float32)
    grad_tokens = (
        cotangent.astype(jnp.float32)
        .at[local_ids]
        .add(jnp.where(usable, d_picked, 0.0))
        .astype(jnp.bfloat16)
    )
    gain_part = jnp.sum(jnp.where(usable, d_normed * scaled, 0.0), axis=0)
    router_part = jnp.sum(d_logit * picked, axis=0)
    grad_gain, grad_router = lax.psum((gain_part, router_part), "context")
    return (mixed, grad_tokens, grad_gate, grad_up, grad_down, grad_gain, grad_router)


def solution(mesh):
    return jax.shard_map(
        body,
        mesh=mesh,
        in_specs=(
            P("context", "tensor"),
            P("tensor"),
            P("tensor"),
            P("tensor", "context"),
            P("tensor", "context"),
            P("context", "tensor"),
            P("context", None),
            P("context"),
            P("context", "tensor"),
        ),
        out_specs=(
            P("context", "tensor"),
            P("context", "tensor"),
            P("tensor", "context"),
            P("tensor", "context"),
            P("context", "tensor"),
            P("tensor"),
            P("tensor"),
        ),
        check_vma=False,
    )
```

profile of v0, /device:TPU:32, one launch (start us, length us, event | category | flops | bytes accessed | tf_op | source)
XLA Modules:
  0.0 901.1 jit_solution(10253769934774257687)
XLA Ops:
  7.2 0.0 copy-start
  7.2 0.0 all-gather.6.cloned.1.call-start
  7.2 1.1 copy.20
  8.3 0.7 compare_select_fusion
  9.0 0.7 compare_and_fusion
  9.6 0.6 gather_fusion
  10.2 0.2 fusion.18
  10.4 14.9 %psum.43 = f32[24]{0:T(128)S(1)} all-reduce(f32[24]{0:T(128)S(1)} %fusion.18), channel_id=1, replica_groups=mesh['context'=32,'tensor'=8] {'tensor'}, use_global_device_ids=true, to_apply=%region_2.4 | all-reduce | flops 24 | bytes 192 | tf_op jit(solution)/shard_map/psum | solution.py:33
  26.0 1.4 fusion.13
  27.4 0.0 all-gather.6.cloned.1.call-update
  27.4 0.0 reduce-scatter.5.cloned.1.call-start
  27.4 76.4 %all-gather.6.cloned.1.call-done = bf16[768,1024]{1,0:T(8,128)(2,1)} async-done(((bf16[24,1024]{1,0:T(8,128)(2,1)}), bf16[768,1024]{1,0:T(8,128)(2,1)}) %all-gather.6.cloned.1.call-update) | async-done | bytes 1572880 | tf_op jit(solution)/shard_map/all_gather | solution.py:44
  103.9 3.9 fusion.36
  107.8 1.8 fusion.37
  109.6 2.9 pad_maximum_fusion
  112.4 0.0 reduce-scatter.5.cloned.1.call-update
  112.5 0.0 all-gather.8.cloned.1.call-start
  112.5 41.5 %reduce-scatter.5.cloned.1.call-done = f32[96,1792]{1,0:T(8,128)} async-done(((f32[768,1792]{1,0:T(8,128)}), f32[96,1792]{1,0:T(8,128)}) %reduce-scatter.5.cloned.1.call-update) | async-done | bytes 688144 | tf_op jit(solution)/shard_map/reduce_scatter | solution.py:45
  154.0 1.9 multiply_convert_fusion.2
  155.9 0.0 all-gather.8.cloned.1.call-update
  155.9 0.0 reduce-scatter.7.cloned.1.call-start
  155.9 27.0 %all-gather.8.cloned.1.call-done = bf16[768,896]{1,0:T(8,128)(2,1)} async-done(((bf16[96,896]{1,0:T(8,128)(2,1)}), bf16[768,896]{1,0:T(8,128)(2,1)}) %all-gather.8.cloned.1.call-update) | async-done | bytes 1376272 | tf_op jit(solution)/shard_map/all_gather | solution.py:60
  182.9 4.3 convolution_convert_fusion.3
  187.2 0.0 reduce-scatter.7.cloned.1.call-update
  187.2 0.0 all-gather.10.cloned.1.call-start
  187.3 0.9 copy-done.2
  188.2 0.6 gather_fusion.1
  188.8 0.0 copy-done.6
  188.8 0.2 convolution_bitcast_fusion
  189.0 213.8 %reduce-scatter.7.cloned.1.call-done = bf16[24,1024]{1,0:T(8,128)(2,1)} async-done(((bf16[768,1024]{1,0:T(8,128)(2,1)}), bf16[24,1024]{1,0:T(8,128)(2,1)}) %reduce-scatter.7.cloned.1.call-update) | async-done | bytes 49168 | tf_op jit(solution)/shard_map/reduce_scatter | solution.py:61
  402.8 1.0 fusion.11
  403.7 12.4 %all-reduce.1 = (f32[24]{0:T(128)S(1)}, f32[24]{0:T(128)S(1)}) all-reduce(f32[24]{0:T(128)S(1)} %convolution_bitcast_fusion, f32[24]{0:T(128)S(1)} %fusion.11), channel_id=1, replica_groups=mesh['context'=32,'tensor'=8] {'tensor'}, use_global_device_ids=true, to_apply=%region_0.0 | all-reduce | flops 48 | bytes 384 | tf_op jit(solution)/shard_map/psum | solution.py:33
  416.2 0.7 fusion.10
  416.9 0.0 all-gather.10.cloned.1.call-update
  416.9 0.0 reduce-scatter.9.cloned.1.call-start
  417.0 73.5 %all-gather.10.cloned.1.call-done = bf16[768,1024]{1,0:T(8,128)(2,1)} async-done(((bf16[24,1024]{1,0:T(8,128)(2,1)}), bf16[768,1024]{1,0:T(8,128)(2,1)}) %all-gather.10.cloned.1.call-update) | async-done | bytes 1572880 | tf_op jit(solution)/shard_map/all_gather | solution.py:71
  490.4 4.8 fusion.38
  495.2 0.0 reduce-scatter.9.cloned.1.call-update
  495.2 0.0 all-gather.12.cloned.1.call-start
  495.3 35.9 %reduce-scatter.9.cloned.1.call-done = f32[96,896]{1,0:T(8,128)} async-done(((f32[768,896]{1,0:T(8,128)}), f32[96,896]{1,0:T(8,128)}) %reduce-scatter.9.cloned.1.call-update) | async-done | bytes 344080 | tf_op jit(solution)/shard_map/reduce_scatter | solution.py:74
  531.2 0.0 copy-done.1
  531.2 1.9 multiply_convert_fusion
  533.1 0.0 all-gather.12.cloned.1.call-update
  533.1 0.0 all-gather.14.cloned.1.call-start
  533.2 0.7 all-gather.14.cloned.1.call-update
  533.9 0.0 reduce-scatter.11.cloned.1.call-start
  533.9 25.4 %all-gather.12.cloned.1.call-done = bf16[768,896]{1,0:T(8,128)(2,1)} async-done(((bf16[96,896]{1,0:T(8,128)(2,1)}), bf16[768,896]{1,0:T(8,128)(2,1)}) %all-gather.12.cloned.1.call-update) | async-done | bytes 1376272 | tf_op jit(solution)/shard_map/all_gather | solution.py:82
  559.3 5.4 fusion.39
  564.7 24.0 %all-gather.14.cloned.1.call-done = bf16[768,896]{1,0:T(8,128)(2,1)} async-done(((bf16[96,896]{1,0:T(8,128)(2,1)}), bf16[768,896]{1,0:T(8,128)(2,1)}) %all-gather.14.cloned.1.call-update) | async-done | bytes 1376272 | tf_op jit(solution)/shard_map/all_gather | solution.py:83
  588.7 5.9 add_convert_fusion
  594.6 0.0 reduce-scatter.11.cloned.1.call-update
  594.7 0.6 copy-done.12
  595.3 0.2 copy-done.4
  595.4 1.1 scatter_custom_fusion
  596.6 0.0 copy-start.3
  596.6 4.8 convolution_convert_fusion
  601.4 3.1 convolution_convert_fusion.1
  604.5 3.1 convolution_convert_fusion.2
  607.6 202.8 %reduce-scatter.11.cloned.1.call-done = bf16[24,1024]{1,0:T(8,128)(2,1)} async-done(((bf16[768,1024]{1,0:T(8,128)(2,1)}), bf16[24,1024]{1,0:T(8,128)(2,1)}) %reduce-scatter.11.cloned.1.call-update) | async-done | bytes 49168 | tf_op jit(solution)/shard_map/reduce_scatter | solution.py:87
  810.4 1.0 fusion.17
  811.4 12.4 %psum.44 = f32[24]{0:T(128)S(1)} all-reduce(f32[24]{0:T(128)S(1)} %get-tuple-element.9), channel_id=1, replica_groups=mesh['context'=32,'tensor'=8] {'tensor'}, use_global_device_ids=true, to_apply=%region_9.11 | all-reduce | flops 24 | bytes 192 | tf_op jit(solution)/shard_map/psum | solution.py:96
  823.8 1.4 scatter_custom_fusion.1
  825.2 0.7 convert_element_type.68
  825.9 68.6 %all-reduce = (f32[1024]{0:T(1024)}, f32[1024]{0:T(1024)}) all-reduce(f32[1024]{0:T(1024)S(1)} %get-tuple-element.8, f32[1024]{0:T(1024)S(1)} %get-tuple-element.10), channel_id=1, replica_groups=mesh['context'=32,'tensor'=8] {'context'}, use_global_device_ids=true, to_apply=%region_14.16 | all-reduce | flops 2048 | bytes 16384 | tf_op jit(solution)/shard_map/psum | solution.py:108
  (28 shorter events, 0.1 us)
Async XLA Ops:
  7.2 175.8 %copy-start = (bf16[896,1024]{1,0:T(8,128)(2,1)S(1)}, bf16[896,1024]{1,0:T(8,128)(2,1)}, u32[]{:S(2)}) copy-start(bf16[896,1024]{1,0:T(8,128)(2,1)} %param.16) | copy-start | bytes 5505028
  7.2 96.7 %all-gather.6.cloned.1.call-start = ((), (), s32[]{:S(2)}) async-start(), calls=%async_computation.4 | async-start | bytes 1622016 | tf_op jit(solution)/shard_map/all_gather | solution.py:44
  27.4 126.6 %reduce-scatter.5.cloned.1.call-start = ((), (), s32[]{:S(2)}) async-start(), calls=%async_computation.5 | async-start | bytes 6193152 | tf_op jit(solution)/shard_map/reduce_scatter | solution.py:45
  103.9 3.9 copy-start.7
  103.9 3.9 copy-start.8
  112.5 70.5 %all-gather.8.cloned.1.call-start = ((), (), s32[]{:S(2)}) async-start(), calls=%async_computation.6 | async-start | bytes 1548288 | tf_op jit(solution)/shard_map/all_gather | solution.py:60
  155.9 246.9 %reduce-scatter.7.cloned.1.call-start = ((), (), s32[]{:S(2)}) async-start(), calls=%async_computation.7 | async-start | bytes 1622016 | tf_op jit(solution)/shard_map/reduce_scatter | solution.py:61
  187.2 0.9 copy-start.2
  187.2 1.6 copy-start.6
  187.2 303.2 %all-gather.10.cloned.1.call-start = ((), (), s32[]{:S(2)}) async-start(), calls=%async_computation.8 | async-start | bytes 1622016 | tf_op jit(solution)/shard_map/all_gather | solution.py:71
  416.9 114.3 %reduce-scatter.9.cloned.1.call-start = ((), (), s32[]{:S(2)}) async-start(), calls=%async_computation.9 | async-start | bytes 3096576 | tf_op jit(solution)/shard_map/reduce_scatter | solution.py:74
  495.2 36.0 %copy-start.1 = (f32[96,1792]{1,0:T(8,128)S(1)}, f32[96,1792]{1,0:T(8,128)}, u32[]{:S(2)}) copy-start(f32[96,1792]{1,0:T(8,128)} %reduce-scatter.5.cloned.1.call-done) | copy-start | bytes 2064388
  495.2 64.1 %all-gather.12.cloned.1.call-start = ((), (), s32[]{:S(2)}) async-start(), calls=%async_computation.10 | async-start | bytes 1548288 | tf_op jit(solution)/shard_map/all_gather | solution.py:82
  533.1 55.6 %all-gather.14.cloned.1.call-start = ((), (), s32[]{:S(2)}) async-start(), calls=%async_computation.11 | async-start | bytes 1548288 | tf_op jit(solution)/shard_map/all_gather | solution.py:83
  533.9 276.5 %reduce-scatter.11.cloned.1.call-start = ((), (), s32[]{:S(2)}) async-start(), calls=%async_computation.12 | async-start | bytes 1622016 | tf_op jit(solution)/shard_map/reduce_scatter | solution.py:87
  594.6 0.7 copy-start.12
  594.6 0.8 copy-start.4
  596.6 4.9 copy-start.3
  596.6 4.9 copy-start.9
  596.6 4.8 copy-start.11
  601.4 3.1 copy-start.10
  604.5 205.9 %copy-start.5 = (f32[1024]{0:T(1024)S(1)}, f32[1024]{0:T(1024)}, u32[]{:S(2)}) copy-start(f32[1024]{0:T(1024)} %param.12) | copy-start | bytes 12292
Sparse Core Ops, SparseCore 0:
  27.5 76.2 all-gather.5
  112.6 41.3 reduce-scatter.4
  156.4 26.4 all-gather.7
  187.4 215.3 reduce-scatter.6
  417.0 73.3 all-gather.9
  495.3 35.8 reduce-scatter.8
  533.8 25.5 all-gather.11
  561.9 26.8 all-gather.13
  594.7 215.5 reduce-scatter.10
where the time goes:
time: 906 us; the launch traced here: 901 us
  waiting for transfers between devices  721 us (80%)
  blocking collectives  108 us (12%)
  matrix products  37.2 us (4%)
  other arithmetic  15.5 us (2%)
  between operations  14.7 us (2%)
    reduce_scatter x1, waiting for transfers between devices, body(): lax.psum_scatter(jnp.dot(hidden_all, w_down, preferred_element_type=jnp.f...  214 us
    reduce_scatter x1, waiting for transfers between devices, body(): lax.psum_scatter((contract_cols(d_gate_all, w_gate) + contract_cols(d_upw...  203 us
    all_gather x1, waiting for transfers between devices, body(): normed_pad = lax.all_gather(normed, 'context', axis=0, tiled=True)  76.4 us
    all_gather x1, waiting for transfers between devices, body(): d_branch_pad = lax.all_gather(d_branch, 'context', axis=0, tiled=True)  73.5 us
    psum x1, blocking collectives, body(): grad_gain, grad_router = lax.psum((gain_part, router_part), 'context')  68.6 us
    reduce_scatter x1, waiting for transfers between devices, body(): lax.psum_scatter(jnp.concatenate([jnp.dot(normed_pad, w_gate, preferred_e...  41.5 us
    reduce_scatter x1, waiting for transfers between devices, body(): lax.psum_scatter(contract_cols(d_branch_pad, w_down), 'tensor', scatter_d...  35.9 us
    psum x2, blocking collectives, body(): lax.psum((jnp.sum(picked * picked, axis=1), jnp.dot(picked_low, router, p...  27.3 us
  transfers between devices with their start and end apart: 9, of which 9 were waited for; matrix products, arithmetic and copies ran while one was open for 2% of the time, Pallas kernels for 0%

commit v1 on v0

v1 whole, which is shorter than its diff:
```python
import jax
import jax.numpy as jnp
from jax import lax
from jax.experimental import pallas as pl
from jax.experimental.pallas import tpu as pltpu
from jax.sharding import PartitionSpec as P

D = 8192
EPS = 1e-05
NX, NZ, NY = 4, 8, 4
SHARDS = NX * NZ
CAP = 24
ROWS = 512
CHUNK = 64
FFL = 896
COLS = 1024
MARK = 1024.0
MESH = pl.DeviceIdType.MESH
VMEM = pltpu.VMEM
F32 = jnp.float32
BF16 = jnp.bfloat16


def contract_rows(left, right):
    return lax.dot_general(left, right, (((0,), (0,)), ((), ())), preferred_element_type=F32)


def contract_cols(left, right):
    return lax.dot_general(left, right, (((1,), (1,)), ((), ())), preferred_element_type=F32)


def dot(left, right):
    return jnp.dot(left, right, preferred_element_type=F32)


class Net:
    def __init__(self, send_sems, recv_sems):
        self.send_sems, self.recv_sems = send_sems, recv_sems
        self.index, self.sent = {}, []

    def make(self, key, src, dst, device):
        k = self.index.setdefault(key, len(self.index))
        return pltpu.make_async_remote_copy(
            src_ref=src,
            dst_ref=dst,
            send_sem=self.send_sems.at[k],
            recv_sem=self.recv_sems.at[k],
            device_id=device,
            device_id_type=MESH,
        )

    def send(self, key, src, dst, device):
        copy = self.make(key, src, dst, device)
        copy.start()
        self.sent.append(copy)

    def arrive(self, key, dst, device):
        self.make(key, dst, dst, device).wait_recv()

    def finish(self):
        for copy in self.sent:
            copy.wait_send()


def enter(partners):
    barrier = pltpu.get_barrier_semaphore()
    for device in partners:
        pl.semaphore_signal(barrier, inc=1, device_id=device, device_id_type=MESH)
    pl.semaphore_wait(barrier, len(partners))


def place():
    c, t = lax.axis_index("context"), lax.axis_index("tensor")
    z, x = lax.div(c, NX), lax.rem(c, NX)

    def at(dz, dx):
        return lax.rem(z + dz + NZ, NZ) * NX + lax.rem(x + dx + NX, NX)

    return t, at


HALF = COLS // 2
QUART = COLS // 4
ORDER = (0, -1, 1, -2, 2, -3, 3, 4)


def gather_kernel(b_ref, g_ref, send_sems, recv_sems):
    t, at = place()
    net = Net(send_sems, recv_sems)

    def dev(dz, dx):
        return (at(dz, dx), t)

    def part(dz, dx, lo, n):
        return g_ref.at[at(dz, dx), :, pl.ds(lo, n)]

    g_ref[at(0, 0)] = b_ref[...]
    enter([dev(0, 1), dev(0, 2), dev(0, 3), dev(1, 0), dev(-1, 0)])

    def a_pass(s, j):
        if s < 4:
            r = part(1 - s, j, 0, HALF)
            net.send(("ar", s, j), r, r, dev(1, 0))
            r = part(s - 1, j, 0, HALF)
            net.send(("al", s, j), r, r, dev(-1, 0))
        else:
            r = part(1 - s, j, 0, QUART)
            net.send(("ar", s, j), r, r, dev(1, 0))
            r = part(s - 1, j, QUART, QUART)
            net.send(("al", s, j), r, r, dev(-1, 0))

    def a_take(s, j):
        if s < 4:
            net.arrive(("ar", s, j), part(-s, j, 0, HALF), dev(-1, 0))
            net.arrive(("al", s, j), part(s, j, 0, HALF), dev(1, 0))
        else:
            net.arrive(("ar", s, j), part(-s, j, 0, QUART), dev(-1, 0))
            net.arrive(("al", s, j), part(s, j, QUART, QUART), dev(1, 0))

    def b_pass(s):
        n = HALF if s < 4 else QUART
        r = part(1 - s, 0, HALF, n)
        net.send(("br", s), r, r, dev(1, 0))
        r = part(s - 1, 0, HALF + HALF - n, n)
        net.send(("bl", s), r, r, dev(-1, 0))

    def b_take(s):
        n = HALF if s < 4 else QUART
        net.arrive(("br", s), part(-s, 0, HALF, n), dev(-1, 0))
        net.arrive(("bl", s), part(s, 0, HALF + HALF - n, n), dev(1, 0))

    def b_side(o):
        r = part(o, 0, HALF, HALF)
        net.send(("xr", o), r, r, dev(0, 1))
        net.send(("xl", o), r, r, dev(0, -1))

    def b_cross(o):
        net.arrive(("xr", o), part(o, -1, HALF, HALF), dev(0, -1))
        r = part(o, -1, HALF, QUART)
        net.send(("dr", o), r, r, dev(0, 1))
        net.arrive(("xl", o), part(o, 1, HALF, HALF), dev(0, 1))
        r = part(o, 1, HALF + QUART, QUART)
        net.send(("dl", o), r, r, dev(0, -1))

    own = part(0, 0, 0, HALF)
    b_pass(1)
    for j in (1, 2, 3):
        net.send(("ax", j), own, own, dev(0, j))
    a_pass(1, 0)
    b_side(0)
    for j in (1, 3, 2):
        net.arrive(("ax", 4 - j), part(0, j, 0, HALF), dev(0, j))
        a_pass(1, j)
    for s in (1, 2, 3, 4):
        b_take(s)
        if s < 4:
            b_pass(s + 1)
            b_side(-s)
            b_side(s)
        else:
            b_side(4)
        for j in (0, 1, 3, 2):
            a_take(s, j)
            if s < 4:
                a_pass(s + 1, j)
        if s == 1:
            b_cross(0)
        else:
            b_cross(1 - s)
            b_cross(s - 1)
    b_cross(4)
    for o in ORDER:
        net.arrive(("dr", o), part(o, 2, HALF, QUART), dev(0, -1))
        net.arrive(("dl", o), part(o, 2, HALF + QUART, QUART), dev(0, 1))
    net.finish()


def gather_shards(block):
    return pl.pallas_call(
        gather_kernel,
        out_shape=jax.ShapeDtypeStruct((SHARDS, 2 * CAP, COLS), BF16),
        in_specs=[pl.BlockSpec(memory_space=VMEM)],
        out_specs=pl.BlockSpec(memory_space=VMEM),
        scratch_shapes=[
            pltpu.SemaphoreType.DMA((80,)),
            pltpu.SemaphoreType.DMA((80,)),
        ],
        compiler_params=pltpu.CompilerParams(
            collective_id=0, has_side_effects=True, vmem_limit_bytes=24 << 20
        ),
        name="gather_shards",
    )(block)


def middle_kernel(
    y_ref, st_ref, h_ref, stat_ref, p_ref,
    r1, acc, rd, rf, st_slots, p_slots, send_sems, recv_sems,
):
    c, t = lax.axis_index("context"), lax.axis_index("tensor")
    y, core = lax.div(t, 2), lax.rem(t, 2)
    net = Net(send_sems, recv_sems)

    def dev(dy, flip=0):
        k = 1 - core if flip else core
        return (c, lax.rem(y + dy + NY, NY) * 2 + k)

    def chunk(dy, flip=0):
        return dev(dy, flip)[1]

    peers = [(dy, f) for dy in range(NY) for f in (0, 1) if (dy, f) != (0, 0)]
    st_slots[t] = st_ref[...]
    enter([dev(dy, f) for dy, f in peers])

    for dy in (2, 1, 3, 0):
        net.send(("c", dy), y_ref.at[chunk(dy, 1)], r1.at[dy], dev(0, 1))
    for dy, f in peers:
        s = st_slots.at[t]
        net.send(("st", dy, f), s, s, dev(dy, f))

    def pair(dy, rows):
        return y_ref[chunk(dy), rows].astype(F32) + r1[dy, rows].astype(F32)

    top, low = pl.ds(0, 32), pl.ds(32, 32)
    net.arrive(("c", 2), r1.at[2], dev(0, 1))
    for i in range(4):
        rows = pl.ds(16 * i, 16)
        acc[2, rows] = pair(2, rows).astype(BF16)
    net.send(("dr",), acc.at[2, top], rd.at[0], dev(1))
    net.send(("dl",), acc.at[2, low], rd.at[1], dev(-1))
    for dy, k, key, plus in ((1, 0, ("dr",), (0, 1)), (3, 1, ("dl",), (2, 3))):
        net.arrive(("c", dy), r1.at[dy], dev(0, 1))
        net.arrive(key, rd.at[k], dev(-1 if dy == 1 else 1))
        for i in range(4):
            rows = pl.ds(16 * i, 16)
            v = pair(dy, rows)
            if i in plus:
                v = v + rd[k, pl.ds(16 * i - 32 * k, 16)].astype(F32)
            acc[dy, rows] = v.astype(BF16)
        net.send(("f", k), acc.at[dy], rf.at[k], dev(1 if dy == 1 else -1))

    for dy, f in peers:
        back = (NY - dy) % NY
        net.arrive(("st", dy, f), st_slots.at[chunk(back, f)], dev(back, f))
    stat = st_slots[0]
    for k in range(1, 8):
        stat = stat + st_slots[k]
    stat_ref[...] = stat
    sub = lax.broadcasted_iota(jnp.int32, (8, 128), 0)
    lane = lax.broadcasted_iota(jnp.int32, (CHUNK, 128), 1)
    row = lax.broadcasted_iota(jnp.int32, (CHUNK, 128), 0)
    mine = lane == row + core * CHUNK

    def column(which):
        line = jnp.sum(jnp.where(sub == which, stat, 0.0), axis=0, keepdims=True)
        return jnp.sum(jnp.where(mine, line, 0.0), axis=1, keepdims=True)

    inv_rms = lax.rsqrt(column(y) / D + EPS)
    weight = jax.nn.sigmoid(column(4 + y))

    net.arrive(("c", 0), r1.at[0], dev(0, 1))
    net.arrive(("f", 0), rf.at[0], dev(-1))
    net.arrive(("f", 1), rf.at[1], dev(1))
    firsts, seconds = [], []
    for i in range(4):
        rows = pl.ds(16 * i, 16)
        inv = inv_rms[16 * i:16 * i + 16]
        w = weight[16 * i:16 * i + 16]

        def total(k):
            cols = pl.ds(k * FFL, FFL)
            return (
                y_ref[t, rows, cols].astype(F32)
                + r1[0, rows, cols].astype(F32)
                + rf[0, rows, cols].astype(F32)
                + rf[1, rows, cols].astype(F32)
            )

        g_raw, u_raw, d_raw = total(0), total(1), total(2)
        gate, upward = g_raw * inv, u_raw * inv
        sigma = jax.nn.sigmoid(gate)
        act = gate * sigma
        hidden = (act * upward * w).astype(BF16)
        d_hidden = d_raw * (w * inv)
        d_gate = (d_hidden * upward * sigma * (1.0 + gate * (1.0 - sigma))).astype(BF16)
        d_up = (d_hidden * act).astype(BF16)
        h_ref[t, rows, pl.ds(0, FFL)] = hidden
        h_ref[t, rows, pl.ds(FFL, FFL)] = d_gate
        h_ref[t, rows, pl.ds(2 * FFL, FFL)] = d_up
        firsts.append(jnp.sum(d_raw * hidden.astype(F32), axis=1, keepdims=True))
        seconds.append(
            jnp.sum(d_gate.astype(F32) * g_raw + d_up.astype(F32) * u_raw, axis=1, keepdims=True)
        )

    own = h_ref.at[t]
    net.send(("gr",), own, own, dev(1))
    net.send(("gl",), own, own, dev(-1))
    net.send(("g", 0), own, own, dev(0, 1))

    def line_of(parts):
        return jnp.sum(jnp.where(mine, jnp.concatenate(parts, axis=0), 0.0), axis=0, keepdims=True)

    p_slots[t] = jnp.where(sub == y, line_of(firsts), 0.0) + jnp.where(
        sub == 4 + y, line_of(seconds), 0.0
    )
    for dy, f in peers:
        s = p_slots.at[t]
        net.send(("p", dy, f), s, s, dev(dy, f))

    net.arrive(("gr",), h_ref.at[chunk(-1)], dev(-1))
    r = h_ref.at[chunk(-1), top]
    net.send(("er",), r, r, dev(1))
    net.arrive(("gl",), h_ref.at[chunk(1)], dev(1))
    r = h_ref.at[chunk(1), low]
    net.send(("el",), r, r, dev(-1))
    for dy in (3, 1):
        r = h_ref.at[chunk(dy)]
        net.send(("g", dy), r, r, dev(0, 1))
    net.arrive(("er",), h_ref.at[chunk(2), top], dev(-1))
    net.arrive(("el",), h_ref.at[chunk(2), low], dev(1))
    r = h_ref.at[chunk(2)]
    net.send(("g", 2), r, r, dev(0, 1))
    for dy, f in peers:
        back = (NY - dy) % NY
        net.arrive(("p", dy, f), p_slots.at[chunk(back, f)], dev(back, f))
    p = p_slots[0]
    for k in range(1, 8):
        p = p + p_slots[k]
    p_ref[...] = p
    for dy in (0, 3, 1, 2):
        net.arrive(("g", dy), h_ref.at[chunk(dy, 1)], dev(0, 1))
    net.finish()


def middle(parts, stats):
    return pl.pallas_call(
        middle_kernel,
        out_shape=(
            jax.ShapeDtypeStruct((8, CHUNK, 3 * FFL), BF16),
            jax.ShapeDtypeStruct((8, 128), F32),
            jax.ShapeDtypeStruct((8, 128), F32),
        ),
        in_specs=[pl.BlockSpec(memory_space=VMEM)] * 2,
        out_specs=(pl.BlockSpec(memory_space=VMEM),) * 3,
        scratch_shapes=[
            VMEM((4, CHUNK, 3 * FFL), BF16),
            VMEM((4, CHUNK, 3 * FFL), BF16),
            VMEM((2, CHUNK // 2, 3 * FFL), BF16),
            VMEM((2, CHUNK, 3 * FFL), BF16),
            VMEM((8, 8, 128), F32),
            VMEM((8, 8, 128), F32),
            pltpu.SemaphoreType.DMA((40,)),
            pltpu.SemaphoreType.DMA((40,)),
        ],
        compiler_params=pltpu.CompilerParams(
            collective_id=1, has_side_effects=True, vmem_limit_bytes=32 << 20
        ),
        name="middle",
    )(parts, stats)


def scatter_kernel(
    v_ref, small_ref, out_ref, tot_ref,
    za, zb, xa, xb, w, sx, sz, send_sems, recv_sems,
):
    t, at = place()
    net = Net(send_sems, recv_sems)

    def dev(dz, dx):
        return (at(dz, dx), t)

    own_x = at(0, 0)
    sx[0] = small_ref[...]
    enter([dev(0, dx) for dx in (1, 2, 3)] + [dev(dz, 0) for dz in range(1, NZ)])

    def mine(dz, dx, lo, n):
        return v_ref[at(dz, dx), :, pl.ds(lo, n)].astype(F32)

    def b_start(i, o):
        far = v_ref.at[at(o, 2), :, pl.ds(HALF, QUART)]
        net.send(("xr1", i), far, xb.at[i, 0, :, pl.ds(0, QUART)], dev(0, 1))
        far = v_ref.at[at(o, 2), :, pl.ds(HALF + QUART, QUART)]
        net.send(("xl1", i), far, xb.at[i, 1, :, pl.ds(QUART, QUART)], dev(0, -1))

    first, second = pl.ds(0, QUART), pl.ds(QUART, QUART)

    def b_next(i, o):
        net.arrive(("xr1", i), xb.at[i, 0, :, first], dev(0, -1))
        xb[i, 0, :, first] = (xb[i, 0, :, first].astype(F32) + mine(o, 1, HALF, QUART)).astype(BF16)
        xb[i, 0, :, second] = v_ref[at(o, 1), :, pl.ds(HALF + QUART, QUART)]
        net.send(("xr2", i), xb.at[i, 0], xb.at[i, 2], dev(0, 1))
        net.arrive(("xl1", i), xb.at[i, 1, :, second], dev(0, 1))
        xb[i, 1, :, second] = (
            xb[i, 1, :, second].astype(F32) + mine(o, -1, HALF + QUART, QUART)
        ).astype(BF16)
        xb[i, 1, :, first] = v_ref[at(o, -1), :, pl.ds(HALF, QUART)]
        net.send(("xl2", i), xb.at[i, 1], xb.at[i, 3], dev(0, -1))

    def b_sum(i, o):
        net.arrive(("xr2", i), xb.at[i, 2], dev(0, -1))
        net.arrive(("xl2", i), xb.at[i, 3], dev(0, 1))
        return mine(o, 0, HALF, HALF) + xb[i, 2].astype(F32) + xb[i, 3].astype(F32)

    def ring_first(tag, k, right, left, buf):
        net.send((tag, "r", 1, k), right, buf.at[0, 0, :, first], dev(1, 0))
        net.send((tag, "l", 1, k), left, buf.at[1, 0, :, second], dev(-1, 0))

    def ring_next(tag, k, s, right, left, buf):
        for d, (name, term, back) in enumerate((("r", right, -1), ("l", left, 1))):
            if s == 2:
                cols, rest = (first, second) if d == 0 else (second, first)
                net.arrive((tag, name, 1, k), buf.at[d, 0, :, cols], dev(back, 0))
                lo = 0 if d == 0 else QUART
                hi = QUART - lo
                buf[d, 0, :, cols] = (
                    buf[d, 0, :, cols].astype(F32) + term[:, lo:lo + QUART]
                ).astype(BF16)
                buf[d, 0, :, rest] = term[:, hi:hi + QUART].astype(BF16)
            else:
                net.arrive((tag, name, s - 1, k), buf.at[d, s - 2], dev(back, 0))
                buf[d, s - 2] = (buf[d, s - 2].astype(F32) + term).astype(BF16)
            net.send((tag, name, s, k), buf.at[d, s - 2], buf.at[d, s - 1], dev(-back, 0))

    def ring_last(tag, k, term, buf):
        net.arrive((tag, "r", 4, k), buf.at[0, 3], dev(-1, 0))
        net.arrive((tag, "l", 4, k), buf.at[1, 3], dev(1, 0))
        return term + buf[0, 3].astype(F32) + buf[1, 3].astype(F32)

    order = (4, 3, -3, 2, -2, 1, -1, 0)
    lanes = (2, 1, 3, 0)
    for i in (0, 1, 2):
        b_start(i, order[i])
    for j in lanes:
        ring_first(
            "a", j,
            v_ref.at[at(4, j), :, pl.ds(0, QUART)],
            v_ref.at[at(4, j), :, pl.ds(QUART, QUART)],
            za.at[j],
        )
    for i in (3, 4, 5, 6, 7):
        b_start(i, order[i])
    for dx in (1, 2, 3):
        net.send(("sx", dx), sx.at[0], sx.at[dx], dev(0, dx))

    for i in (0, 1, 2):
        b_next(i, order[i])
    for j in lanes:
        ring_next("a", j, 2, mine(3, j, 0, HALF), mine(-3, j, 0, HALF), za.at[j])
    for i in (3, 4, 5, 6, 7):
        b_next(i, order[i])

    for dx in (1, 2, 3):
        net.arrive(("sx", dx), sx.at[dx], dev(0, -dx))
    sz[0] = sx[0] + sx[1] + sx[2] + sx[3]
    for dz in range(1, NZ):
        net.send(("sz", dz), sz.at[0], sz.at[dz], dev(dz, 0))

    w[...] = b_sum(0, 4).astype(BF16)
    ring_first("b", 0, w.at[:, first], w.at[:, second], zb)
    for j in lanes:
        ring_next("a", j, 3, mine(2, j, 0, HALF), mine(-2, j, 0, HALF), za.at[j])
    ring_next("b", 0, 2, b_sum(1, 3), b_sum(2, -3), zb)
    for j in lanes:
        ring_next("a", j, 4, mine(1, j, 0, HALF), mine(-1, j, 0, HALF), za.at[j])
    ring_next("b", 0, 3, b_sum(3, 2), b_sum(4, -2), zb)
    for j in (2, 1, 3):
        v = ring_last("a", j, mine(0, j, 0, HALF), za.at[j])
        xa[j, 0] = v.astype(BF16)
        net.send(("xa", j), xa.at[j, 0], xa.at[j, 1], dev(0, j))
    ring_next("b", 0, 4, b_sum(5, 1), b_sum(6, -1), zb)
    v = ring_last("a", 0, mine(0, 0, 0, HALF), za.at[0])
    for j in (1, 3, 2):
        net.arrive(("xa", j), xa.at[j, 1], dev(0, -j))
        v = v + xa[j, 1].astype(F32)
    out_ref[:, pl.ds(0, HALF)] = v
    out_ref[:, pl.ds(HALF, HALF)] = ring_last("b", 0, b_sum(7, 0), zb)
    for dz in range(1, NZ):
        net.arrive(("sz", dz), sz.at[dz], dev(-dz, 0))
    tot = sz[0]
    for dz in range(1, NZ):
        tot = tot + sz[dz]
    tot_ref[...] = tot
    net.finish()


def scatter_sums(values, small):
    n = 2 * CAP
    return pl.pallas_call(
        scatter_kernel,
        out_shape=(
            jax.ShapeDtypeStruct((n, COLS), F32),
            jax.ShapeDtypeStruct((16, 128), F32),
        ),
        in_specs=[pl.BlockSpec(memory_space=VMEM)] * 2,
        out_specs=(pl.BlockSpec(memory_space=VMEM),) * 2,
        scratch_shapes=[
            VMEM((4, 2, 4, n, HALF), BF16),
            VMEM((2, 4, n, HALF), BF16),
            VMEM((4, 2, n, HALF), BF16),
            VMEM((8, 4, n, HALF), BF16),
            VMEM((n, HALF), BF16),
            VMEM((4, 16, 128), F32),
            VMEM((8, 16, 128), F32),
            pltpu.SemaphoreType.DMA((96,)),
            pltpu.SemaphoreType.DMA((96,)),
        ],
        compiler_params=pltpu.CompilerParams(
            collective_id=2, has_side_effects=True, vmem_limit_bytes=32 << 20
        ),
        name="scatter_sums",
    )(values, small)


def body(tokens, norm_gain, router, w_gate, w_up, w_down, routes, counts, cotangent):
    live_count = counts[0]
    usable = (jnp.arange(CAP, dtype=jnp.int32) < live_count)[:, None]
    local_ids = routes[0]
    picked_low = jnp.take(tokens, local_ids, axis=0)
    slope_low = jnp.take(cotangent, local_ids, axis=0)
    block = jnp.concatenate(
        [jnp.where(usable, picked_low, jnp.asarray(MARK, BF16)), slope_low], axis=0
    )
    blocks = gather_shards(block)
    x_pad = blocks[:, :CAP].reshape(SHARDS * CAP, COLS)
    s_pad = blocks[:, CAP:].reshape(SHARDS * CAP, COLS)
    live = x_pad[:, 0].astype(F32) < 0.5 * MARK
    spot = jnp.cumsum(live.astype(jnp.int32)) - 1
    spot = jnp.where(live, spot, -1)
    select = (spot[None, :] == jnp.arange(ROWS, dtype=jnp.int32)[:, None]).astype(BF16)
    x_all = dot(select, x_pad).astype(BF16)
    s_all = dot(select, s_pad).astype(BF16)
    x_f32 = x_all.astype(F32)
    normed = (x_f32 * norm_gain).astype(BF16)
    sums = jnp.concatenate(
        [
            dot(normed, w_gate).astype(BF16),
            dot(normed, w_up).astype(BF16),
            contract_cols(s_all, w_down).astype(BF16),
        ],
        axis=1,
    )
    stats = jnp.concatenate(
        [
            jnp.sum(x_f32 * x_f32, axis=1),
            jnp.sum(x_f32 * router.astype(F32), axis=1),
        ]
    ).reshape(8, 128)
    acts, stats, inner = middle(sums.reshape(8, CHUNK, 3 * FFL), stats)
    acts = acts.reshape(ROWS, 3 * FFL)
    hidden, d_gate, d_up = acts[:, :FFL], acts[:, FFL:2 * FFL], acts[:, 2 * FFL:]
    branch = dot(hidden, w_down)
    d_normed = contract_cols(d_gate, w_gate) + contract_cols(d_up, w_up)
    gain_part = jnp.sum(d_normed * x_f32, axis=0)
    values = jnp.concatenate(
        [
            contract_rows(select, branch.astype(BF16)).astype(BF16).reshape(SHARDS, CAP, COLS),
            contract_rows(select, d_normed.astype(BF16)).astype(BF16).reshape(SHARDS, CAP, COLS),
        ],
        axis=1,
    )
    small = jnp.concatenate([inner, gain_part.reshape(8, 128)], axis=0)
    ends, small = scatter_sums(values, small)
    grad_down = contract_rows(hidden, s_all).astype(BF16)
    grad_gate = contract_rows(normed, d_gate).astype(BF16)
    grad_up = contract_rows(normed, d_up).astype(BF16)

    inv_sq = 1.0 / (stats[:4].reshape(ROWS) / D + EPS)
    weight = jax.nn.sigmoid(stats[4:].reshape(ROWS))
    d_logit = small[:4].reshape(ROWS) * (1.0 - weight)
    mean_term = small[4:8].reshape(ROWS) / D * inv_sq
    grad_gain = small[8:].reshape(COLS)
    grad_router = jnp.sum(d_logit[:, None] * x_f32, axis=0)
    own = lax.dynamic_slice(spot, (lax.axis_index("context") * CAP,), (CAP,))
    own = jnp.maximum(own, 0)
    d_logit = jnp.take(d_logit, own)[:, None]
    mean_term = jnp.take(mean_term, own)[:, None]
    picked = picked_low.astype(F32)
    mixed_rows = (picked + ends[:CAP]).astype(BF16)
    mixed = tokens.at[local_ids].set(jnp.where(usable, mixed_rows, picked_low))
    d_picked = ends[CAP:] * norm_gain - picked * mean_term + d_logit * router.astype(F32)
    grad_rows = (slope_low.astype(F32) + d_picked).astype(BF16)
    grad_tokens = cotangent.at[local_ids].set(jnp.where(usable, grad_rows, slope_low))
    return (mixed, grad_tokens, grad_gate, grad_up, grad_down, grad_gain, grad_router)


def solution(mesh):
    return jax.shard_map(
        body,
        mesh=mesh,
        in_specs=(
            P("context", "tensor"),
            P("tensor"),
            P("tensor"),
            P("tensor", "context"),
            P("tensor", "context"),
            P("context", "tensor"),
            P("context", None),
            P("context"),
            P("context", "tensor"),
        ),
        out_specs=(
            P("context", "tensor"),
            P("context", "tensor"),
            P("tensor", "context"),
            P("tensor", "context"),
            P("context", "tensor"),
            P("tensor"),
            P("tensor"),
        ),
        check_vma=False,
    )
```

time: 906 us -> 144 us (0.16)
  waiting for transfers between devices: 721 us -> 0 us
  blocking collectives: 108 us -> 0 us
  Pallas kernels: 0 us -> 104 us
  matrix products: 37.2 us -> 21.6 us
  between operations: 14.7 us -> 1.62 us
  other arithmetic: 15.5 us -> 5.52 us
    reduce_scatter x4 -> x0, waiting for transfers between devices: 494 us -> none  [the longest x1 214 us: body(): lax.psum_scatter(jnp.dot(hidden_all, w_down, preferred_element_type=jnp.f...]
    all_gather x5 -> x0, waiting for transfers between devices: 226 us -> none  [the longest x1 76.4 us: body(): normed_pad = lax.all_gather(normed, 'context', axis=0, tiled=True)]
    psum x4 -> x0, blocking collectives: 108 us -> none  [the longest x1 68.6 us: body(): grad_gain, grad_router = lax.psum((gain_part, router_part), 'context')]
    pallas_call x0 -> x3, Pallas kernels: none -> 104 us  [the longest x1 36.6 us: middle(): pl.pallas_call(middle_kernel, out_shape=(jax.ShapeDtypeStruct((8, CHUNK,...]
    dot_general x3, matrix products: 16 us -> 3.94 us  [contract_cols(): lax.dot_general(left, right, (((1,), (1,)), ((), ())), preferred_element_...]
  transfers between devices with their start and end apart: 9 -> 0, of which waited for: 9 -> 0; matrix products, arithmetic and copies ran while one was open for 2% -> 0% of each run, Pallas kernels for 0% -> 0%
where the time goes in v1:
time: 144 us; the launch traced here: 143 us
  Pallas kernels  104 us (72%)
  matrix products  21.6 us (15%)
  local copies, waits for them, and re-layouts  10.4 us (7%)
  other arithmetic  5.52 us (4%)
  between operations  1.62 us (1%)
    pallas_call x1, Pallas kernels, middle(): pl.pallas_call(middle_kernel, out_shape=(jax.ShapeDtypeStruct((8, CHUNK,...  36.6 us
    pallas_call x1, Pallas kernels, gather_shards(): pl.pallas_call(gather_kernel, out_shape=jax.ShapeDtypeStruct((SHARDS, 2 *...  35.5 us
    pallas_call x1, Pallas kernels, scatter_sums(): pl.pallas_call(scatter_kernel, out_shape=(jax.ShapeDtypeStruct((n, COLS),...  32 us
    dot_general x5, matrix products, contract_rows(): lax.dot_general(left, right, (((0,), (0,)), ((), ())), preferred_element_...  13 us
    unnamed x43, local copies, waits for them, and re-layouts  4.72 us
    dot_general x4, matrix products, dot(): return jnp.dot(left, right, preferred_element_type=F32)  4.66 us
    dot_general x3, matrix products, contract_cols(): lax.dot_general(left, right, (((1,), (1,)), ((), ())), preferred_element_...  3.94 us

profile of v1, /device:TPU:32, one launch (start us, length us, event | category | flops | bytes accessed | tf_op | source)
XLA Modules:
  0.0 143.3 jit_solution(1652089688355065960)
XLA Ops:
  0.6 0.0 copy-start
  0.6 1.1 copy.23
  1.7 1.0 copy.24
  2.8 0.7 compare_select_fusion
  3.4 0.6 gather_fusion
  4.7 0.7 compare_and_fusion
  5.4 0.6 gather_fusion.1
  6.0 0.1 broadcast_select_fusion.2
  6.1 0.0 copy-done.3
  6.1 0.0 copy-done.6
  6.1 35.5 %gather_shards.1 = bf16[32,48,1024]{2,1,0:T(8,128)(2,1)S(1)} custom-call(bf16[48,1024]{1,0:T(8,128)(2,1)S(1)} %pad_maximum_fusion.2.b_ref), custom_call_target="tpu_custom_call" | custom-call | tf_op jit(solution)/shard_map/gather_shards/pallas_call | solution.py:179
  41.6 0.0 copy-start.14
  41.6 1.5 %fusion.46 = (bf16[32,24,1024]{2,1,0:T(8,128)(2,1)S(1)}, bf16[32,24,1024]{2,1,0:T(8,128)(2,1)}) fusion(bf16[32,48,1024]{2,1,0:T(8,128)(2,1)S(1)} %gather_shards.1), kind=kLoop, calls=%fused_computation.87 | loop fusion | bytes 6291456 | tf_op jit(solution)/shard_map/slice | solution.py:523
  43.1 0.7 slice.69
  43.8 1.0 copy.17
  44.9 0.3 reduce-window.9
  45.2 0.1 slice.48
  45.3 0.1 slice_reduce_fusion
  45.4 0.1 bitcast_select_fusion
  45.5 0.0 copy-done.14
  45.5 1.2 fusion.1
  46.7 0.2 copy-done.9
  46.9 1.0 fusion.8
  47.9 0.0 copy-done
  47.9 0.0 copy-start.18
  48.0 0.0 copy-start.13
  48.0 0.0 copy-start.17
  48.0 1.3 convolution_convert_fusion.6
  49.3 0.0 copy-done.18
  49.3 0.0 copy-done.13
  49.3 0.5 copy-done.17
  49.9 1.3 convolution_convert_fusion.7
  51.1 0.2 copy-done.16
  51.3 1.3 convolution_convert_fusion.8
  52.6 0.2 pad_maximum_fusion.1
  52.8 36.6 %middle.1 = (bf16[8,64,2688]{2,1,0:T(8,128)(2,1)S(1)}, f32[8,128]{1,0:T(8,128)S(1)}, f32[8,128]{1,0:T(8,128)S(1)}) custom-call(bf16[8,64,2688]{2,1,0:T(8,128)(2,1)S(1)} %bitcast.39, f32[8,128]{1,0:T(8,128)S(1)} %pad_maximum_fusion.4.st_ref), custom_call_target="tpu_custom_call" | custom-call | tf_op jit(solution)/shard_map/middle/pallas_call | solution.py:335
  89.5 0.0 copy-start.1
  89.5 1.3 fusion.13
  90.8 0.0 copy-done.11
  90.8 0.3 copy-done.1
  91.0 1.3 fusion.3
  92.4 4.4 %convolution_convert_fusion.4 = bf16[768,1024]{1,0:T(8,128)(2,1)} fusion(bf16[896,1024]{1,0:T(8,128)(2,1)S(1)} %copy-done, bf16[512,2688]{1,0:T(8,128)(2,1)} %bitcast.42, s32[768]{0:T(1024)S(1)} %bitcast_select_fusion), kind=kOutput, calls=%fused_computation.22 | convolution fusion | flops 1746534400 | bytes 4328448 | tf_op jit(solution)/shard_map/dot_general | solution.py:25
  96.8 1.2 convolution_convert_fusion.3
  98.0 0.2 copy-done.10
  98.2 0.4 pad_maximum_fusion.v_ref
  98.6 0.0 copy-start.2
  98.7 0.0 copy-start.19
  98.7 32.0 %scatter_sums.1 = (f32[48,1024]{1,0:T(8,128)S(1)}, f32[16,128]{1,0:T(8,128)S(1)}) custom-call(bf16[32,48,1024]{2,1,0:T(8,128)(2,1)S(1)} %pad_maximum_fusion.v_ref, f32[16,128]{1,0:T(8,128)S(1)} %pad_maximum_fusion.3.small_ref), custom_call_target="tpu_custom_call" | custom-call | tf_op jit(solution)/shard_map/scatter_sums/pallas_call | solution.py:487
  130.7 0.9 fusion.4
  131.6 0.0 copy-done.19
  131.6 2.4 %convolution_convert_fusion = bf16[896,1024]{1,0:T(8,128)(2,1)} fusion(bf16[512,1024]{1,0:T(8,128)(2,1)S(1)} %copy-done.19, bf16[512,2688]{1,0:T(8,128)(2,1)S(1)} %bitcast.43), kind=kOutput, calls=%fused_computation.18 | convolution fusion | flops 940441600 | bytes 3801088 | tf_op jit(solution)/shard_map/dot_general | solution.py:25
  134.0 2.5 %convolution_convert_fusion.1 = bf16[1024,896]{1,0:T(8,128)(2,1)} fusion(bf16[512,2688]{1,0:T(8,128)(2,1)S(1)} %bitcast.44, bf16[512,1024]{1,0:T(8,128)(2,1)S(1)} %copy-done.12, f32[1024]{0:T(1024)S(1)} %copy-done.13), kind=kOutput, calls=%fused_computation.19 | convolution fusion | flops 942014464 | bytes 3805184 | tf_op jit(solution)/shard_map/dot_general | solution.py:25
  136.5 2.5 %convolution_convert_fusion.2 = bf16[1024,896]{1,0:T(8,128)(2,1)} fusion(bf16[512,2688]{1,0:T(8,128)(2,1)S(1)} %bitcast.45, bf16[512,1024]{1,0:T(8,128)(2,1)S(1)} %copy-done.12, f32[1024]{0:T(1024)S(1)} %copy-done.13), kind=kOutput, calls=%fused_computation.20 | convolution fusion | flops 942014464 | bytes 3805184 | tf_op jit(solution)/shard_map/dot_general | solution.py:25
  139.0 0.1 dynamic-slice_maximum_fusion
  139.1 0.7 gather_fusion.3
  139.8 0.7 gather_fusion.2
  140.6 0.1 compare_select_fusion.3
  140.6 0.0 copy-done.15
  140.6 1.0 scatter_custom_fusion.1
  141.6 0.0 copy-start.8
  141.7 1.0 scatter_custom_fusion
  142.6 0.0 copy-start.5
  142.6 0.6 slice_bitcast_fusion
  143.3 0.0 copy-done.5
  (26 shorter events, 0.2 us)
Async XLA Ops:
  0.6 47.3 %copy-start = (bf16[896,1024]{1,0:T(8,128)(2,1)S(1)}, bf16[896,1024]{1,0:T(8,128)(2,1)}, u32[]{:S(2)}) copy-start(bf16[896,1024]{1,0:T(8,128)(2,1)} %param.18) | copy-start | bytes 5505028
  1.7 4.4 %copy-start.3 = (bf16[128,1024]{1,0:T(8,128)(2,1)}, bf16[128,1024]{1,0:T(8,128)(2,1)S(1)}, u32[]{:S(2)}) copy-start(bf16[128,1024]{1,0:T(8,128)(2,1)S(1)} %copy.23) | copy-start | bytes 786436
  2.8 3.3 %copy-start.6 = (bf16[128,1024]{1,0:T(8,128)(2,1)}, bf16[128,1024]{1,0:T(8,128)(2,1)S(1)}, u32[]{:S(2)}) copy-start(bf16[128,1024]{1,0:T(8,128)(2,1)S(1)} %copy.24) | copy-start | bytes 786436
  41.6 3.9 %copy-start.14 = (bf16[1024]{0:T(1024)(128)(2,1)S(1)}, bf16[1024]{0:T(1024)(128)(2,1)}, u32[]{:S(2)}) copy-start(bf16[1024]{0:T(1024)(128)(2,1)} %param.15) | copy-start | bytes 6148
  45.5 1.4 copy-start.9
  46.7 44.1 %copy-start.11 = (bf16[512,1024]{1,0:T(8,128)(2,1)}, bf16[512,1024]{1,0:T(8,128)(2,1)S(1)}, u32[]{:S(2)}) copy-start(bf16[512,1024]{1,0:T(8,128)(2,1)S(1)} %get-tuple-element.29) | copy-start | bytes 3145732
  47.9 1.4 copy-start.18
  48.0 1.4 copy-start.13
  48.0 1.9 %copy-start.17 = (bf16[1024,896]{1,0:T(8,128)(2,1)S(1)}, bf16[1024,896]{1,0:T(8,128)(2,1)}, u32[]{:S(2)}) copy-start(bf16[1024,896]{1,0:T(8,128)(2,1)} %param.17) | copy-start | bytes 5505028
  49.8 1.5 %copy-start.16 = (bf16[1024,896]{1,0:T(8,128)(2,1)S(1)}, bf16[1024,896]{1,0:T(8,128)(2,1)}, u32[]{:S(2)}) copy-start(bf16[1024,896]{1,0:T(8,128)(2,1)} %param.16) | copy-start | bytes 5505028
  89.5 1.6 %copy-start.1 = (bf16[8,64,2688]{2,1,0:T(8,128)(2,1)}, bf16[8,64,2688]{2,1,0:T(8,128)(2,1)S(1)}, u32[]{:S(2)}) copy-start(bf16[8,64,2688]{2,1,0:T(8,128)(2,1)S(1)} %get-tuple-element.14) | copy-start | bytes 8257540
  96.8 1.4 copy-start.10
  98.2 32.5 %copy-start.12 = (bf16[512,1024]{1,0:T(8,128)(2,1)S(1)}, bf16[512,1024]{1,0:T(8,128)(2,1)}, u32[]{:S(2)}) copy-start(bf16[512,1024]{1,0:T(8,128)(2,1)} %copy-done.11) | copy-start | bytes 3145732
  98.6 33.0 %copy-start.2 = (bf16[8,64,2688]{2,1,0:T(8,128)(2,1)S(1)}, bf16[8,64,2688]{2,1,0:T(8,128)(2,1)}, u32[]{:S(2)}) copy-start(bf16[8,64,2688]{2,1,0:T(8,128)(2,1)} %copy-done.1) | copy-start | bytes 8257540
  98.7 33.0 %copy-start.19 = (bf16[512,1024]{1,0:T(8,128)(2,1)S(1)}, bf16[512,1024]{1,0:T(8,128)(2,1)}, u32[]{:S(2)}) copy-start(bf16[512,1024]{1,0:T(8,128)(2,1)} %copy-done.18) | copy-start | bytes 3145732
  136.5 4.1 %copy-start.15 = (s32[1,24]{1,0:T(1,128)S(1)}, s32[1,24]{1,0:T(1,128)}, u32[]{:S(2)}) copy-start(s32[1,24]{1,0:T(1,128)} %param.19) | copy-start | bytes 292
  136.5 4.1 %copy-start.7 = (bf16[128,1024]{1,0:T(8,128)(2,1)S(1)}, bf16[128,1024]{1,0:T(8,128)(2,1)}, u32[]{:S(2)}) copy-start(bf16[128,1024]{1,0:T(8,128)(2,1)} %copy-done.6) | copy-start | bytes 786436
  136.5 5.1 %copy-start.4 = (bf16[128,1024]{1,0:T(8,128)(2,1)S(1)}, bf16[128,1024]{1,0:T(8,128)(2,1)}, u32[]{:S(2)}) copy-start(bf16[128,1024]{1,0:T(8,128)(2,1)} %copy-done.3) | copy-start | bytes 786436
  141.6 1.6 %copy-start.8 = (bf16[128,1024]{1,0:T(8,128)(2,1)}, bf16[128,1024]{1,0:T(8,128)(2,1)S(1)}, u32[]{:S(2)}) copy-start(bf16[128,1024]{1,0:T(8,128)(2,1)S(1)} %scatter_custom_fusion.1) | copy-start | bytes 786436
  142.6 0.7 copy-start.5

commit v2 on v0

v2 whole, which is shorter than its diff:
```python
import jax
import jax.numpy as jnp
from jax import lax
from jax.experimental import pallas as pl
from jax.experimental.pallas import tpu as pltpu
from jax.sharding import PartitionSpec as P

D = 8192
EPS = 1e-05
NX, NZ, NY = 4, 8, 4
SHARDS = NX * NZ
CAP = 24
SLOTS = SHARDS * CAP
ROWS = 512
CHUNK = 64
FFL = 896
COLS = 1024
TALL, WIDE = 2 * CAP, COLS // 2
HALF, QUART = WIDE // 2, WIDE // 4
MARK = 1024.0
SEMS = 320
MESH = pl.DeviceIdType.MESH
VMEM = pltpu.VMEM
F32 = jnp.float32
BF16 = jnp.bfloat16
FF_TILES = ((0, 256), (256, 256), (512, 256), (768, 128))
COL_TILES = ((0, 256), (256, 256), (512, 256), (768, 256))


def contract_rows(left, right):
    return lax.dot_general(left, right, (((0,), (0,)), ((), ())), preferred_element_type=F32)


def contract_cols(left, right):
    return lax.dot_general(left, right, (((1,), (1,)), ((), ())), preferred_element_type=F32)


def dot(left, right):
    return jnp.dot(left, right, preferred_element_type=F32)


class Net:
    def __init__(self, send_sems, recv_sems):
        self.send_sems, self.recv_sems = send_sems, recv_sems
        self.index, self.sent = {}, []

    def make(self, key, src, dst, device):
        k = self.index.setdefault(key, len(self.index))
        assert k < SEMS
        return pltpu.make_async_remote_copy(
            src_ref=src,
            dst_ref=dst,
            send_sem=self.send_sems.at[k],
            recv_sem=self.recv_sems.at[k],
            device_id=device,
            device_id_type=MESH,
        )

    def send(self, key, src, dst, device):
        copy = self.make(key, src, dst, device)
        copy.start()
        self.sent.append(copy)

    def arrive(self, key, dst, device):
        self.make(key, dst, dst, device).wait_recv()

    def finish(self):
        for copy in self.sent:
            copy.wait_send()


class Place:
    def __init__(self):
        self.c, self.t = lax.axis_index("context"), lax.axis_index("tensor")
        self.z, self.x = lax.div(self.c, NX), lax.rem(self.c, NX)
        self.y, self.core = lax.div(self.t, 2), lax.rem(self.t, 2)
        self.odd = lax.rem(self.x, 2)
        self.pair = lax.div(self.x, 2)

    def at_z(self, dz):
        return lax.rem(self.z + dz + NZ, NZ)

    def at(self, dz, dx):
        return self.at_z(dz) * NX + lax.rem(self.x + dx + NX, NX)

    def dev(self, dz, dx):
        return (self.at(dz, dx), self.t)

    def mate(self, q):
        if q == 1:
            return self.x + 1 - 2 * self.odd
        return lax.rem(self.x + 2, NX) if q == 2 else 3 - self.x

    def mate_at(self, q):
        return self.z * NX + self.mate(q)

    def mate_dev(self, q):
        return (self.mate_at(q), self.t)

    def pair_at(self, dz, other):
        p = 1 - self.pair if other else self.pair
        return pl.ds(self.at_z(dz) * NX + 2 * p, 2)

    def chunk(self, dy, flip=0):
        k = 1 - self.core if flip else self.core
        return lax.rem(self.y + dy + NY, NY) * 2 + k

    def peer(self, dy, flip=0):
        return (self.c, self.chunk(dy, flip))


PEERS = [(dy, f) for dy in range(NY) for f in (0, 1) if (dy, f) != (0, 0)]


class Gather:
    def __init__(self, tag, net, me, g):
        self.tag, self.net, self.me, self.g = tag, net, me, g

    def part(self, dz, dx, lo, n):
        return self.g.at[self.me.at(dz, dx), :, pl.ds(lo, n)]

    def duo(self, dz, other, lo, n):
        return self.g.at[self.me.pair_at(dz, other), :, pl.ds(lo, n)]

    def send(self, key, ref, device):
        self.net.send((self.tag,) + key, ref, ref, device)

    def arrive(self, key, ref, device):
        self.net.arrive((self.tag,) + key, ref, device)

    def spans(self, s):
        return ((0, HALF), (0, HALF)) if s < 4 else ((0, QUART), (QUART, QUART))

    def a_pass(self, s, other):
        right, left = self.spans(s)
        self.send(("ar", s, other), self.duo(1 - s, other, *right), self.me.dev(1, 0))
        self.send(("al", s, other), self.duo(s - 1, other, *left), self.me.dev(-1, 0))

    def a_take(self, s, other):
        right, left = self.spans(s)
        self.arrive(("ar", s, other), self.duo(-s, other, *right), self.me.dev(-1, 0))
        self.arrive(("al", s, other), self.duo(s, other, *left), self.me.dev(1, 0))

    def b_pass(self, s):
        (r, n), (l, _) = self.spans(s)
        self.send(("br", s), self.part(1 - s, 0, HALF + r, n), self.me.dev(1, 0))
        self.send(("bl", s), self.part(s - 1, 0, HALF + l, n), self.me.dev(-1, 0))

    def b_take(self, s):
        (r, n), (l, _) = self.spans(s)
        self.arrive(("br", s), self.part(-s, 0, HALF + r, n), self.me.dev(-1, 0))
        self.arrive(("bl", s), self.part(s, 0, HALF + l, n), self.me.dev(1, 0))

    def b_side(self, o):
        r = self.part(o, 0, HALF, HALF)
        self.send(("xr", o), r, self.me.dev(0, 1))
        self.send(("xl", o), r, self.me.dev(0, -1))

    def b_cross(self, o):
        self.arrive(("xr", o), self.part(o, -1, HALF, HALF), self.me.dev(0, -1))
        self.send(("dr", o), self.part(o, -1, HALF, QUART), self.me.dev(0, 1))
        self.arrive(("xl", o), self.part(o, 1, HALF, HALF), self.me.dev(0, 1))
        self.send(("dl", o), self.part(o, 1, HALF + QUART, QUART), self.me.dev(0, -1))

    def start(self):
        own = self.part(0, 0, 0, HALF)
        for q in (1, 2, 3):
            self.send(("ax", q), own, self.me.mate_dev(q))
        self.b_pass(1)
        self.b_side(0)

    def begin_ring(self):
        for q in (1, 2, 3):
            ref = self.g.at[self.me.mate_at(q), :, pl.ds(0, HALF)]
            self.arrive(("ax", q), ref, self.me.mate_dev(q))
            if q != 2:
                self.a_pass(1, int(q == 3))

    def step(self, s):
        self.b_take(s)
        if s < 4:
            self.b_pass(s + 1)
            self.b_side(-s)
            self.b_side(s)
        else:
            self.b_side(4)
        for other in (0, 1):
            self.a_take(s, other)
            if s < 4:
                self.a_pass(s + 1, other)
        for o in ((0,) if s == 1 else (1 - s, s - 1)):
            self.b_cross(o)

    def drain(self):
        self.b_cross(4)
        for o in (0, -1, 1, -2, 2, -3, 3, 4):
            self.arrive(("dr", o), self.part(o, 2, HALF, QUART), self.me.dev(0, -1))
            self.arrive(("dl", o), self.part(o, 2, HALF + QUART, QUART), self.me.dev(0, 1))


class Scatter:
    ORDER = (4, 3, -3, 2, -2, 1, -1, 0)

    def __init__(self, tag, net, me, v, za, zb, xa, xb, fin, w):
        self.tag, self.net, self.me, self.v = tag, net, me, v
        self.za, self.zb, self.xa, self.xb, self.fin, self.w = za, zb, xa, xb, fin, w

    def send(self, key, src, dst, device):
        self.net.send((self.tag,) + key, src, dst, device)

    def arrive(self, key, ref, device):
        self.net.arrive((self.tag,) + key, ref, device)

    def mine(self, dz, dx, lo, n):
        return self.v[self.me.at(dz, dx), :, pl.ds(lo, n)].astype(F32)

    def duo(self, dz, other):
        return self.v[self.me.pair_at(dz, other), :, pl.ds(0, HALF)].astype(F32)

    def b_start(self, i):
        o = self.ORDER[i]
        k = self.me.at(o, 2)
        self.send(("xr1", i), self.v.at[k, :, pl.ds(HALF, QUART)],
                  self.xb.at[i, 0, :, pl.ds(0, QUART)], self.me.dev(0, 1))
        self.send(("xl1", i), self.v.at[k, :, pl.ds(HALF + QUART, QUART)],
                  self.xb.at[i, 1, :, pl.ds(QUART, QUART)], self.me.dev(0, -1))

    def b_next(self, i):
        o, xb = self.ORDER[i], self.xb
        first, second = pl.ds(0, QUART), pl.ds(QUART, QUART)
        self.arrive(("xr1", i), xb.at[i, 0, :, first], self.me.dev(0, -1))
        term = self.mine(o, 1, HALF, HALF)
        xb[i, 0, :, first] = (xb[i, 0, :, first].astype(F32) + term[:, :QUART]).astype(BF16)
        xb[i, 0, :, second] = term[:, QUART:].astype(BF16)
        self.send(("xr2", i), xb.at[i, 0], xb.at[i, 2], self.me.dev(0, 1))
        self.arrive(("xl1", i), xb.at[i, 1, :, second], self.me.dev(0, 1))
        term = self.mine(o, -1, HALF, HALF)
        xb[i, 1, :, second] = (xb[i, 1, :, second].astype(F32) + term[:, QUART:]).astype(BF16)
        xb[i, 1, :, first] = term[:, :QUART].astype(BF16)
        self.send(("xl2", i), xb.at[i, 1], xb.at[i, 3], self.me.dev(0, -1))

    def b_sum(self, i):
        self.arrive(("xr2", i), self.xb.at[i, 2], self.me.dev(0, -1))
        self.arrive(("xl2", i), self.xb.at[i, 3], self.me.dev(0, 1))
        return (self.mine(self.ORDER[i], 0, HALF, HALF)
                + self.xb[i, 2].astype(F32) + self.xb[i, 3].astype(F32))

    def ring_first(self, k, right, left, buf):
        self.send(("r", 1, k), right, buf.at[0, 0, ..., pl.ds(0, QUART)], self.me.dev(1, 0))
        self.send(("l", 1, k), left, buf.at[1, 0, ..., pl.ds(QUART, QUART)], self.me.dev(-1, 0))

    def ring_next(self, k, s, right, left, buf):
        for d, (name, term, back) in enumerate((("r", right, -1), ("l", left, 1))):
            if s == 2:
                lo = d * QUART
                hi = QUART - lo
                cols = pl.ds(lo, QUART)
                self.arrive((name, 1, k), buf.at[d, 0, ..., cols], self.me.dev(back, 0))
                buf[d, 0, ..., cols] = (
                    buf[d, 0, ..., cols].astype(F32) + term[..., lo:lo + QUART]
                ).astype(BF16)
                buf[d, 0, ..., pl.ds(hi, QUART)] = term[..., hi:hi + QUART].astype(BF16)
            else:
                self.arrive((name, s - 1, k), buf.at[d, s - 2], self.me.dev(back, 0))
                buf[d, s - 2] = (buf[d, s - 2].astype(F32) + term).astype(BF16)
            self.send((name, s, k), buf.at[d, s - 2], buf.at[d, s - 1], self.me.dev(-back, 0))

    def ring_last(self, k, term, buf):
        self.arrive(("r", 4, k), buf.at[0, 3], self.me.dev(-1, 0))
        self.arrive(("l", 4, k), buf.at[1, 3], self.me.dev(1, 0))
        return term + buf[0, 3].astype(F32) + buf[1, 3].astype(F32)

    def a_ring(self, s):
        for other in (1, 0):
            self.ring_next(other, s, self.duo(5 - s, other), self.duo(s - 5, other),
                           self.za.at[other])

    def start(self):
        for i in range(4):
            self.b_start(i)
        for other in (1, 0):
            k = self.me.pair_at(4, other)
            self.ring_first(other, self.v.at[k, :, pl.ds(0, QUART)],
                            self.v.at[k, :, pl.ds(QUART, QUART)], self.za.at[other])
        for i in range(4, 8):
            self.b_start(i)

    def turn(self):
        for i in range(3):
            self.b_next(i)
        self.a_ring(2)
        for i in range(3, 8):
            self.b_next(i)

    def second(self):
        self.w[...] = self.b_sum(0).astype(BF16)
        self.ring_first("b", self.w.at[:, pl.ds(0, QUART)], self.w.at[:, pl.ds(QUART, QUART)], self.zb)
        self.a_ring(3)
        self.ring_next("b", 2, self.b_sum(1), self.b_sum(2), self.zb)

    def third(self):
        self.a_ring(4)
        self.ring_next("b", 3, self.b_sum(3), self.b_sum(4), self.zb)

    def fourth(self):
        me, odd = self.me, self.me.odd
        for other in (1, 0):
            total = self.ring_last(other, self.duo(0, other), self.za.at[other])
            self.fin[other] = total.astype(BF16)
        for q, other, k in ((3, 1, 1 - odd), (2, 1, odd), (1, 0, 1 - odd)):
            self.send(("xa", q), self.fin.at[other, k], self.xa.at[q], me.mate_dev(q))
        self.ring_next("b", 4, self.b_sum(5), self.b_sum(6), self.zb)

    def last(self):
        total = self.fin[0, self.me.odd].astype(F32)
        for q in (1, 3, 2):
            self.arrive(("xa", q), self.xa.at[q], self.me.mate_dev(q))
            total = total + self.xa[q].astype(F32)
        return total, self.ring_last("b", self.b_sum(7), self.zb)


class Unit:
    def __init__(self, net, me, y, h, r1, acc, rd, rf):
        self.net, self.me, self.y, self.h = net, me, y, h
        self.r1, self.acc, self.rd, self.rf = r1, acc, rd, rf

    def pair(self, k, dy):
        return self.y[k, self.me.chunk(dy)].astype(F32) + self.r1[k, dy].astype(F32)

    def share(self, k):
        for dy in (2, 1, 3, 0):
            self.net.send(("c", k, dy), self.y.at[k, self.me.chunk(dy, 1)], self.r1.at[k, dy],
                          self.me.peer(0, 1))

    def far(self, k):
        self.net.arrive(("c", k, 2), self.r1.at[k, 2], self.me.peer(0, 1))
        self.acc[k, 2] = self.pair(k, 2).astype(BF16)
        self.net.send(("dr", k), self.acc.at[k, 2, pl.ds(0, 32)], self.rd.at[k, 0], self.me.peer(1))
        self.net.send(("dl", k), self.acc.at[k, 2, pl.ds(32, 32)], self.rd.at[k, 1], self.me.peer(-1))

    def near(self, k):
        for dy, i, key, back in ((1, 0, "dr", -1), (3, 1, "dl", 1)):
            self.net.arrive(("c", k, dy), self.r1.at[k, dy], self.me.peer(0, 1))
            v = self.pair(k, dy)
            self.net.arrive((key, k), self.rd.at[k, i], self.me.peer(back))
            lo = 32 * i
            hi = 32 - lo
            self.acc[k, dy, pl.ds(lo, 32)] = (
                v[lo:lo + 32] + self.rd[k, i].astype(F32)
            ).astype(BF16)
            self.acc[k, dy, pl.ds(hi, 32)] = v[hi:hi + 32].astype(BF16)
            self.net.send(("f", k, i), self.acc.at[k, dy], self.rf.at[k, i], self.me.peer(-back))

    def settle(self, k):
        self.net.arrive(("c", k, 0), self.r1.at[k, 0], self.me.peer(0, 1))
        self.net.arrive(("f", k, 0), self.rf.at[k, 0], self.me.peer(-1))
        self.net.arrive(("f", k, 1), self.rf.at[k, 1], self.me.peer(1))

    def total(self, k, rows):
        return (
            self.y[k, self.me.t, rows].astype(F32)
            + self.r1[k, 0, rows].astype(F32)
            + self.rf[k, 0, rows].astype(F32)
            + self.rf[k, 1, rows].astype(F32)
        )

    def spread(self, k):
        own = self.h.at[k, self.me.t]
        self.net.send(("gr", k), own, own, self.me.peer(1))
        self.net.send(("gl", k), own, own, self.me.peer(-1))
        self.net.send(("g", k, 0), own, own, self.me.peer(0, 1))

    def relay(self, k):
        me = self.me
        for key, onward, dy, lo in (("gr", "er", -1, 0), ("gl", "el", 1, 32)):
            ref = self.h.at[k, me.chunk(dy)]
            self.net.arrive((key, k), ref, me.peer(dy))
            half = self.h.at[k, me.chunk(dy), pl.ds(lo, 32)]
            self.net.send((onward, k), half, half, me.peer(-dy))
            self.net.send(("g", k, dy), ref, ref, me.peer(0, 1))

    def close(self, k):
        me = self.me
        self.net.arrive(("er", k), self.h.at[k, me.chunk(2), pl.ds(0, 32)], me.peer(-1))
        self.net.arrive(("el", k), self.h.at[k, me.chunk(2), pl.ds(32, 32)], me.peer(1))
        ref = self.h.at[k, me.chunk(2)]
        self.net.send(("g", k, 2), ref, ref, me.peer(0, 1))
        for dy in (0, -1, 1, 2):
            self.net.arrive(("g", k, dy), self.h.at[k, me.chunk(dy, 1)], me.peer(0, 1))


def block_kernel(
    xb_ref, sb_ref, gain_ref, router_ref, wg_hbm, wu_hbm, wd_hbm,
    mix_ref, gt_ref, tot_ref, gr_ref, gg_hbm, gu_hbm, gd_hbm,
    wg, wu, wd, gx, gs, pad, low, up, spot, sel, sel_t, x_all, x_gain, s_all,
    y, h, r1, acc, rd, rf, st_slots, p_slots, prod, vb, vn,
    za_b, zb_b, xa_b, xb_b, fin_b, w_b, za_n, zb_n, xa_n, xb_n, fin_n, w_n,
    sx, sz, go, local_sems, send_sems, recv_sems,
):
    me = Place()
    net = Net(send_sems, recv_sems)
    loads = [
        pltpu.make_async_copy(src, dst, local_sems.at[i])
        for i, (src, dst) in enumerate(((wg_hbm, wg), (wu_hbm, wu), (wd_hbm, wd)))
    ]
    for load in loads:
        load.start()
    gx[me.c] = xb_ref[...]
    gs[me.c] = sb_ref[...]
    barrier = pltpu.get_barrier_semaphore()
    friends = (
        [me.dev(dz, 0) for dz in range(1, NZ)]
        + [me.dev(0, dx) for dx in range(1, NX)]
        + [me.peer(dy, f) for dy, f in PEERS]
    )
    for device in friends:
        pl.semaphore_signal(barrier, inc=1, device_id=device, device_id_type=MESH)
    pl.semaphore_wait(barrier, len(friends))

    gather_x = Gather("X", net, me, gx)
    gather_s = Gather("S", net, me, gs)
    unit = Unit(net, me, y, h, r1, acc, rd, rf)

    gather_x.start()
    for i in range(6):
        rows = pl.ds(128 * i, 128)
        r = lax.broadcasted_iota(jnp.int32, (128, SLOTS), 0) + 128 * i
        k = lax.broadcasted_iota(jnp.int32, (128, SLOTS), 1)
        same = jnp.where(r == k, MARK, 0.0)
        low[rows] = jnp.where(k < r, 1.0, same).astype(BF16)
        up[rows] = jnp.where(r < k, 1.0, same).astype(BF16)
    gather_x.begin_ring()
    for s in (1, 2, 3):
        gather_x.step(s)
    gather_s.start()
    gather_x.step(4)
    gather_x.drain()
    gather_s.begin_ring()

    def flatten(g):
        @pl.loop(0, NZ)
        def _(i):
            v = g[pl.ds(NX * i, NX)].astype(F32)
            rows = pl.ds(pl.multiple_of(i * (NX * CAP), 32), NX * CAP)
            pad[rows, pl.ds(0, WIDE)] = v[:, :CAP].reshape(NX * CAP, WIDE).astype(BF16)
            pad[rows, pl.ds(WIDE, WIDE)] = v[:, CAP:].reshape(NX * CAP, WIDE).astype(BF16)

    flatten(gx)
    live = jnp.where(pad[:, pl.ds(0, 128)].astype(F32)[:, 0:1] < 0.5 * MARK, 1.0, 0.0)
    live = jnp.broadcast_to(live, (SLOTS, 128)).astype(BF16)
    spot[...] = dot(low[...], live) - MARK
    line = contract_rows(live, up[...])[0:1] - MARK
    sel[...] = jnp.where(
        line == lax.broadcasted_iota(jnp.int32, (ROWS, SLOTS), 0).astype(F32), 1.0, 0.0
    ).astype(BF16)
    sq = jnp.zeros((ROWS, 128), F32)
    lg = jnp.zeros((ROWS, 128), F32)
    for lo, n in COL_TILES:
        cols = pl.ds(lo, n)
        v = dot(sel[...], pad[:, cols])
        x_all[:, cols] = v.astype(BF16)
        x_gain[:, cols] = (v * gain_ref[:, cols]).astype(BF16)
        s2, rl = v * v, v * router_ref[:, cols]
        for a in range(0, n, 128):
            sq = sq + s2[:, a:a + 128]
            lg = lg + rl[:, a:a + 128]
    sq = jnp.sum(sq, axis=1, keepdims=True)
    lg = jnp.sum(lg, axis=1, keepdims=True)
    eye = lax.broadcasted_iota(jnp.int32, (128, 128), 0) == lax.broadcasted_iota(
        jnp.int32, (128, 128), 1
    )
    for i in range(8):
        v = (sq, lg)[i // 4][128 * (i % 4):128 * (i % 4) + 128]
        st_slots[me.t, pl.ds(i, 1)] = jnp.sum(jnp.where(eye, v, 0.0), axis=0, keepdims=True)
    for dy, f in PEERS:
        s = st_slots.at[me.t]
        net.send(("st", dy, f), s, s, me.peer(dy, f))

    gather_s.step(1)
    loads[0].wait()
    for lo, n in FF_TILES:
        v = dot(x_gain[...], wg[:, pl.ds(lo, n)])
        y[0, :, :, pl.ds(lo, n)] = v.astype(BF16).reshape(8, CHUNK, n)
    unit.share(0)
    gather_s.step(2)
    loads[1].wait()
    for lo, n in FF_TILES:
        v = dot(x_gain[...], wu[:, pl.ds(lo, n)])
        y[1, :, :, pl.ds(lo, n)] = v.astype(BF16).reshape(8, CHUNK, n)
    unit.share(1)
    unit.far(0)
    gather_s.step(3)
    unit.far(1)
    sel_t[...] = jnp.where(
        jnp.concatenate([spot[...]] * 4, axis=1)
        == lax.broadcasted_iota(jnp.int32, (SLOTS, ROWS), 1).astype(F32), 1.0, 0.0
    ).astype(BF16)
    gather_s.step(4)
    unit.near(0)
    gather_s.drain()
    flatten(gs)
    for lo, n in COL_TILES:
        cols = pl.ds(lo, n)
        s_all[:, cols] = dot(sel[...], pad[:, cols]).astype(BF16)
    unit.near(1)
    loads[2].wait()
    for lo, n in FF_TILES:
        v = contract_cols(s_all[...], wd[pl.ds(lo, n), :])
        y[2, :, :, pl.ds(lo, n)] = v.astype(BF16).reshape(8, CHUNK, n)
    unit.share(2)
    unit.far(2)

    for dy, f in PEERS:
        back = (NY - dy) % NY
        net.arrive(("st", dy, f), st_slots.at[me.chunk(back, f)], me.peer(back, f))
    stat = st_slots[0]
    for k in range(1, 8):
        stat = stat + st_slots[k]
    sub = lax.broadcasted_iota(jnp.int32, (8, 128), 0)
    lane = lax.broadcasted_iota(jnp.int32, (CHUNK, 128), 1)
    row = lax.broadcasted_iota(jnp.int32, (CHUNK, 128), 0)
    at_own = lane == row + me.core * CHUNK

    def column(which):
        line = jnp.sum(jnp.where(sub == which, stat, 0.0), axis=0, keepdims=True)
        return jnp.sum(jnp.where(at_own, line, 0.0), axis=1, keepdims=True)

    inv_rms = lax.rsqrt(column(me.y) / D + EPS)
    weight = jax.nn.sigmoid(column(4 + me.y))
    unit.near(2)
    for k in range(3):
        unit.settle(k)
    firsts, seconds = [], []
    for i in range(4):
        rows = pl.ds(16 * i, 16)
        inv = inv_rms[16 * i:16 * i + 16]
        w = weight[16 * i:16 * i + 16]
        g_raw, u_raw, d_raw = unit.total(0, rows), unit.total(1, rows), unit.total(2, rows)
        gate, upward = g_raw * inv, u_raw * inv
        sigma = jax.nn.sigmoid(gate)
        act = gate * sigma
        hidden = (act * upward * w).astype(BF16)
        d_hidden = d_raw * (w * inv)
        d_gate = (d_hidden * upward * sigma * (1.0 + gate * (1.0 - sigma))).astype(BF16)
        d_up = (d_hidden * act).astype(BF16)
        h[0, me.t, rows] = hidden
        h[1, me.t, rows] = d_gate
        h[2, me.t, rows] = d_up
        firsts.append(jnp.sum(d_raw * hidden.astype(F32), axis=1, keepdims=True))
        seconds.append(
            jnp.sum(d_gate.astype(F32) * g_raw + d_up.astype(F32) * u_raw, axis=1, keepdims=True)
        )
    for k in range(3):
        unit.spread(k)

    def line_of(parts):
        return jnp.sum(jnp.where(at_own, jnp.concatenate(parts, axis=0), 0.0), axis=0, keepdims=True)

    p_slots[me.t] = jnp.where(sub == me.y, line_of(firsts), 0.0) + jnp.where(
        sub == 4 + me.y, line_of(seconds), 0.0
    )
    for dy, f in PEERS:
        s = p_slots.at[me.t]
        net.send(("p", dy, f), s, s, me.peer(dy, f))

    scatter_b = Scatter("B", net, me, vb, za_b, zb_b, xa_b, xb_b, fin_b, w_b)
    scatter_n = Scatter("N", net, me, vn, za_n, zb_n, xa_n, xb_n, fin_n, w_n)

    def all_rows(k):
        return h[k].reshape(ROWS, FFL)

    def expand(v):
        for g in range(2):
            s = sel_t[pl.ds(384 * g, 384), :]
            parts = [
                dot(s, prod[:, pl.ds(WIDE * i, WIDE)]).reshape(16, CAP, WIDE) for i in range(2)
            ]
            v[pl.ds(16 * g, 16)] = jnp.concatenate(parts, axis=1).astype(BF16)

    unit.relay(0)
    unit.close(0)
    for lo, n in COL_TILES:
        cols = pl.ds(lo, n)
        prod[:, cols] = dot(all_rows(0), wd[:, cols]).astype(BF16)
    unit.relay(1)
    expand(vb)
    scatter_b.start()
    unit.relay(2)
    unit.close(1)
    scatter_b.turn()
    unit.close(2)
    for i, (lo, n) in enumerate(COL_TILES):
        cols = pl.ds(lo, n)
        v = contract_cols(all_rows(1), wg[cols, :]) + contract_cols(all_rows(2), wu[cols, :])
        prod[:, cols] = v.astype(BF16)
        line = jnp.sum(v * x_all[:, cols].astype(F32), axis=0, keepdims=True)
        sx[0, pl.ds(8 + 2 * i, 1)] = line[:, :128]
        sx[0, pl.ds(9 + 2 * i, 1)] = line[:, 128:]
    for dy, f in PEERS:
        back = (NY - dy) % NY
        net.arrive(("p", dy, f), p_slots.at[me.chunk(back, f)], me.peer(back, f))
    p = p_slots[0]
    for k in range(1, 8):
        p = p + p_slots[k]
    sx[0, pl.ds(0, 8)] = p
    for dx in (1, 2, 3):
        net.send(("sx", dx), sx.at[0], sx.at[dx], me.dev(0, dx))
    scatter_b.second()
    expand(vn)
    scatter_n.start()
    scatter_b.third()
    for dx in (1, 2, 3):
        net.arrive(("sx", dx), sx.at[dx], me.dev(0, -dx))
    sz[0] = sx[0] + sx[1] + sx[2] + sx[3]
    for dz in range(1, NZ):
        net.send(("sz", dz), sz.at[0], sz.at[dz], me.dev(dz, 0))

    scatter_n.turn()
    scatter_b.fourth()
    stores = []

    def write(i, src, out):
        store = pltpu.make_async_copy(src, out, local_sems.at[3 + i])
        store.start()
        stores.append(store)

    for lo in range(0, FFL, 128):
        left = h[0, :, :, pl.ds(lo, 128)].reshape(ROWS, 128)
        go[0, pl.ds(lo, 128), :] = contract_rows(left, s_all[...]).astype(BF16)
    write(0, go.at[0, pl.ds(0, FFL)], gd_hbm)
    scatter_n.second()
    for lo in range(0, COLS, 256):
        left = x_gain[:, pl.ds(lo, 256)]
        go[1, pl.ds(lo, 256), pl.ds(0, FFL)] = contract_rows(left, all_rows(1)).astype(BF16)
    write(1, go.at[1, :, pl.ds(0, FFL)], gg_hbm)
    scatter_n.third()
    for lo in range(0, COLS, 256):
        left = x_gain[:, pl.ds(lo, 256)]
        go[2, pl.ds(lo, 256), pl.ds(0, FFL)] = contract_rows(left, all_rows(2)).astype(BF16)
    write(2, go.at[2, :, pl.ds(0, FFL)], gu_hbm)
    branch_a, branch_b = scatter_b.last()
    scatter_n.fourth()

    for dz in range(1, NZ):
        net.arrive(("sz", dz), sz.at[dz], me.dev(-dz, 0))
    tot = sz[0]
    for dz in range(1, NZ):
        tot = tot + sz[dz]
    tot_ref[...] = tot
    d_logit = tot[0:4] * (1.0 - jax.nn.sigmoid(stat[4:8]))
    mean_term = tot[4:8] / D / (stat[0:4] / D + EPS)

    def flat(v):
        return jnp.concatenate([v[i:i + 1] for i in range(4)], axis=1)

    d_logit, mean_term = flat(d_logit), flat(mean_term)
    first = d_logit.astype(BF16)
    rest = d_logit - first.astype(F32)
    second = rest.astype(BF16)
    third = (rest - second.astype(F32)).astype(BF16)
    for lo, n in COL_TILES:
        cols = pl.ds(lo, n)
        x = x_all[:, cols]
        gr_ref[:, cols] = dot(first, x) + dot(second, x) + dot(third, x)
    own = spot[pl.ds(pl.multiple_of(me.c * CAP, 8), CAP), :]
    own = jnp.concatenate([own] * 4, axis=1)
    hit = own == lax.broadcasted_iota(jnp.int32, (CAP, ROWS), 1).astype(F32)
    d_logit = jnp.sum(jnp.where(hit, d_logit, 0.0), axis=1, keepdims=True)
    mean_term = jnp.sum(jnp.where(hit, mean_term, 0.0), axis=1, keepdims=True)

    normed_a, normed_b = scatter_n.last()
    for at, branch, d_normed in ((0, branch_a, normed_a), (HALF, branch_b, normed_b)):
        cols = pl.ds(at, HALF)
        picked = xb_ref[:, cols].astype(F32)
        slope = sb_ref[:, cols].astype(F32)
        mix_ref[:, cols] = picked + branch
        for i in range(2):
            r = slice(CAP * i, CAP * i + CAP)
            feats = pl.ds(WIDE * i + at, HALF)
            gt_ref[pl.ds(CAP * i, CAP), cols] = slope[r] + (
                d_normed[r] * gain_ref[:, feats] - picked[r] * mean_term
                + d_logit * router_ref[:, feats]
            )
    for store in stores:
        store.wait()
    net.finish()


def block(x_block, s_block, gain, router, w_gate, w_up, w_down):
    vm = pl.BlockSpec(memory_space=VMEM)
    hbm = pl.BlockSpec(memory_space=pl.ANY)
    ring = [
        VMEM((2, 2, 4, 2, TALL, HALF), BF16),
        VMEM((2, 4, TALL, HALF), BF16),
        VMEM((4, TALL, HALF), BF16),
        VMEM((8, 4, TALL, HALF), BF16),
        VMEM((2, 2, TALL, HALF), BF16),
        VMEM((TALL, HALF), BF16),
    ]
    return pl.pallas_call(
        block_kernel,
        out_shape=(
            jax.ShapeDtypeStruct((TALL, WIDE), F32),
            jax.ShapeDtypeStruct((TALL, WIDE), F32),
            jax.ShapeDtypeStruct((16, 128), F32),
            jax.ShapeDtypeStruct((1, COLS), F32),
            jax.ShapeDtypeStruct((COLS, FFL), BF16),
            jax.ShapeDtypeStruct((COLS, FFL), BF16),
            jax.ShapeDtypeStruct((FFL, COLS), BF16),
        ),
        in_specs=[vm] * 4 + [hbm] * 3,
        out_specs=(vm,) * 4 + (hbm,) * 3,
        scratch_shapes=[
            VMEM((COLS, FFL), BF16),
            VMEM((COLS, FFL), BF16),
            VMEM((FFL, COLS), BF16),
            VMEM((SHARDS, TALL, WIDE), BF16),
            VMEM((SHARDS, TALL, WIDE), BF16),
            VMEM((SLOTS, COLS), BF16),
            VMEM((SLOTS, SLOTS), BF16),
            VMEM((SLOTS, SLOTS), BF16),
            VMEM((SLOTS, 128), F32),
            VMEM((ROWS, SLOTS), BF16),
            VMEM((SLOTS, ROWS), BF16),
            VMEM((ROWS, COLS), BF16),
            VMEM((ROWS, COLS), BF16),
            VMEM((ROWS, COLS), BF16),
            VMEM((3, 8, CHUNK, FFL), BF16),
            VMEM((3, 8, CHUNK, FFL), BF16),
            VMEM((3, 4, CHUNK, FFL), BF16),
            VMEM((3, 4, CHUNK, FFL), BF16),
            VMEM((3, 2, CHUNK // 2, FFL), BF16),
            VMEM((3, 2, CHUNK, FFL), BF16),
            VMEM((8, 8, 128), F32),
            VMEM((8, 8, 128), F32),
            VMEM((ROWS, COLS), BF16),
            VMEM((SHARDS, TALL, WIDE), BF16),
            VMEM((SHARDS, TALL, WIDE), BF16),
            *ring,
            *ring,
            VMEM((4, 16, 128), F32),
            VMEM((8, 16, 128), F32),
            VMEM((3, COLS, COLS), BF16),
            pltpu.SemaphoreType.DMA((6,)),
            pltpu.SemaphoreType.DMA((SEMS,)),
            pltpu.SemaphoreType.DMA((SEMS,)),
        ],
        compiler_params=pltpu.CompilerParams(
            collective_id=0, has_side_effects=True, vmem_limit_bytes=56 << 20
        ),
        name="block",
    )(x_block, s_block, gain, router, w_gate, w_up, w_down)


def fold(rows):
    return jnp.concatenate([rows[:, :WIDE], rows[:, WIDE:]], axis=0)


def unfold(rows):
    return jnp.concatenate([rows[:CAP], rows[CAP:]], axis=1)


def body(tokens, norm_gain, router, w_gate, w_up, w_down, routes, counts, cotangent):
    usable = (jnp.arange(CAP, dtype=jnp.int32) < counts[0])[:, None]
    local_ids = routes[0]
    picked = jnp.take(tokens, local_ids, axis=0)
    slope = jnp.take(cotangent, local_ids, axis=0)
    mixed_rows, grad_rows, sums, grad_router, grad_gate, grad_up, grad_down = block(
        fold(jnp.where(usable, picked, jnp.asarray(MARK, BF16))),
        fold(slope),
        norm_gain[None, :],
        router.astype(F32)[None, :],
        w_gate,
        w_up,
        w_down,
    )
    mixed_rows = jnp.where(usable, unfold(mixed_rows).astype(BF16), picked)
    grad_rows = jnp.where(usable, unfold(grad_rows).astype(BF16), slope)
    mixed = tokens.at[local_ids].set(mixed_rows)
    grad_tokens = cotangent.at[local_ids].set(grad_rows)
    return (
        mixed, grad_tokens, grad_gate, grad_up, grad_down,
        sums[8:].reshape(COLS), grad_router.reshape(COLS),
    )


def solution(mesh):
    return jax.shard_map(
        body,
        mesh=mesh,
        in_specs=(
            P("context", "tensor"),
            P("tensor"),
            P("tensor"),
            P("tensor", "context"),
            P("tensor", "context"),
            P("context", "tensor"),
            P("context", None),
            P("context"),
            P("context", "tensor"),
        ),
        out_specs=(
            P("context", "tensor"),
            P("context", "tensor"),
            P("tensor", "context"),
            P("tensor", "context"),
            P("context", "tensor"),
            P("tensor"),
            P("tensor"),
        ),
        check_vma=False,
    )
```

time: 906 us -> 141 us (0.16)
  waiting for transfers between devices: 721 us -> 0 us
  Pallas kernels: 0 us -> 120 us
  blocking collectives: 108 us -> 0 us
  matrix products: 37.2 us -> 0 us
  between operations: 14.7 us -> 1.38 us
    reduce_scatter x4 -> x0, waiting for transfers between devices: 494 us -> none  [the longest x1 214 us: body(): lax.psum_scatter(jnp.dot(hidden_all, w_down, preferred_element_type=jnp.f...]
    all_gather x5 -> x0, waiting for transfers between devices: 226 us -> none  [the longest x1 76.4 us: body(): normed_pad = lax.all_gather(normed, 'context', axis=0, tiled=True)]
    pallas_call x0 -> x1, Pallas kernels: none -> 120 us  [block(): pl.pallas_call(block_kernel, out_shape=(jax.ShapeDtypeStruct((TALL, WIDE)...]
    psum x4 -> x0, blocking collectives: 108 us -> none  [the longest x1 68.6 us: body(): grad_gain, grad_router = lax.psum((gain_part, router_part), 'context')]
    dot_general x10 -> x0, matrix products: 37.2 us -> none  [the longest x3 16 us: contract_cols(): lax.dot_general(left, right, (((1,), (1,)), ((), ())), preferred_element_...]
  transfers between devices with their start and end apart: 9 -> 0, of which waited for: 9 -> 0; matrix products, arithmetic and copies ran while one was open for 2% -> 0% of each run, Pallas kernels for 0% -> 0%
where the time goes in v2:
time: 141 us
  Pallas kernels  120 us (85%)
  local copies, waits for them, and re-layouts  11.4 us (8%)
  other arithmetic  8.31 us (6%)
    pallas_call x1, Pallas kernels, block(): pl.pallas_call(block_kernel, out_shape=(jax.ShapeDtypeStruct((TALL, WIDE)...  120 us
    unnamed x16, local copies, waits for them, and re-layouts  8.9 us

profile of v2, /device:TPU:32, one launch (start us, length us, event | category | flops | bytes accessed | tf_op | source)
XLA Modules:
  0.0 140.9 jit_solution(8188711236546149042)
XLA Ops:
  0.6 1.0 copy.26
  1.6 0.9 copy.25
  3.2 0.7 compare_and_fusion
  3.9 0.7 fusion.8
  4.5 0.7 compare_select_fusion
  5.2 1.3 broadcast_in_dim.49
  6.5 0.6 gather_fusion
  7.1 0.6 gather_fusion.1
  7.7 0.1 broadcast_select_fusion
  7.8 0.6 pad_maximum_fusion.1.sb_ref
  8.4 0.6 pad_maximum_fusion.xb_ref
  9.0 119.8 %block.1 = (f32[48,512]{1,0:T(8,128)}, f32[48,512]{1,0:T(8,128)}, f32[16,128]{1,0:T(8,128)}, f32[1,1024]{1,0:T(1,128)}, bf16[1024,896]{1,0:T(8,128)(2,1)}, /*ind...) custom-call(bf16[48,512]{1,0:T(8,128)(2,1)} %pad_maximum_fusion.xb_ref, bf16[48,512]{1,0:T(8,128)(2,1)} %pad_maximum_fusion.1.sb_ref, ...), custom_call_target="tpu_custom_call" | custom-call | tf_op jit(solution)/shard_map/block/pallas_call | solution.py:700
  128.8 0.9 convert.13
  129.7 1.0 scatter_custom_fusion
  130.7 0.0 copy-start.3
  130.7 1.3 slice_bitcast_fusion
  132.0 0.9 convert.14
  132.9 1.0 scatter_custom_fusion.1
  133.9 0.0 copy-start.2
  133.9 0.0 copy-start.1
  133.9 3.0 %copy.27 = bf16[1024,896]{1,0:T(8,128)(2,1)} copy(bf16[1024,896]{1,0:T(8,128)(2,1)} %get-tuple-element.43) | data formatting | bytes 3670016
  136.9 0.0 copy-done.3
  136.9 0.0 copy-done.2
  136.9 0.0 copy-done.1
  136.9 0.0 copy-start
  136.9 1.2 copy.28
  138.1 0.9 copy-done
  139.1 0.0 copy-start.4
  139.1 1.2 copy.29
  140.3 0.0 copy-done.4
  140.3 0.6 copy.30
  (5 shorter events, 0.0 us)
Async XLA Ops:
  130.7 6.2 %copy-start.3 = (bf16[128,1024]{1,0:T(8,128)(2,1)}, bf16[128,1024]{1,0:T(8,128)(2,1)S(1)}, u32[]{:S(2)}) copy-start(bf16[128,1024]{1,0:T(8,128)(2,1)S(1)} %scatter_custom_fusion) | copy-start | bytes 786436
  133.9 3.0 %copy-start.2 = (bf16[128,1024]{1,0:T(8,128)(2,1)}, bf16[128,1024]{1,0:T(8,128)(2,1)S(1)}, u32[]{:S(2)}) copy-start(bf16[128,1024]{1,0:T(8,128)(2,1)S(1)} %scatter_custom_fusion.1) | copy-start | bytes 786436
  133.9 3.0 %copy-start.1 = (bf16[1024,896]{1,0:T(8,128)(2,1)S(1)}, bf16[1024,896]{1,0:T(8,128)(2,1)}, u32[]{:S(2)}) copy-start(bf16[1024,896]{1,0:T(8,128)(2,1)} %get-tuple-element.44) | copy-start | bytes 5505028
  136.9 2.2 %copy-start = (bf16[896,1024]{1,0:T(8,128)(2,1)S(1)}, bf16[896,1024]{1,0:T(8,128)(2,1)}, u32[]{:S(2)}) copy-start(bf16[896,1024]{1,0:T(8,128)(2,1)} %get-tuple-element.45) | copy-start | bytes 5505028
  139.1 1.2 copy-start.4

commit v3 on v2

v3 whole, which is shorter than its diff:
```python
import jax
import jax.numpy as jnp
from jax import lax
from jax.experimental import pallas as pl
from jax.experimental.pallas import tpu as pltpu
from jax.sharding import PartitionSpec as P

D = 8192
EPS = 1e-05
NX, NZ, NY = 4, 8, 4
SHARDS = NX * NZ
CAP = 24
SLOTS = SHARDS * CAP
ROWS = 512
CHUNK = 64
FFL = 896
COLS = 1024
TALL, WIDE = 2 * CAP, COLS // 2
SEND_SEMS, RECV_SEMS = 16, 232
MESH = pl.DeviceIdType.MESH
VMEM = pltpu.VMEM
F32 = jnp.float32
BF16 = jnp.bfloat16
FF_TILES = ((0, 256), (256, 256), (512, 256), (768, 128))
COL_TILES = ((0, 256), (256, 256), (512, 256), (768, 256))


def contract_rows(left, right):
    return lax.dot_general(left, right, (((0,), (0,)), ((), ())), preferred_element_type=F32)


def contract_cols(left, right):
    return lax.dot_general(left, right, (((1,), (1,)), ((), ())), preferred_element_type=F32)


def dot(left, right):
    return jnp.dot(left, right, preferred_element_type=F32)


class Net:
    def __init__(self, send_sems, recv_sems, other):
        self.send_sems, self.recv_sems, self.other = send_sems, recv_sems, other
        self.keys, self.groups = {}, {}

    def make(self, key, group, src, dst, device):
        k = self.keys.setdefault(key, len(self.keys))
        g = self.groups.setdefault(group, len(self.groups))
        assert k < RECV_SEMS and g < SEND_SEMS
        return pltpu.make_async_remote_copy(
            src_ref=src,
            dst_ref=dst,
            send_sem=self.send_sems.at[g],
            recv_sem=self.recv_sems.at[k],
            device_id=device,
            device_id_type=MESH,
        )

    def send(self, key, group, src, dst, device):
        self.make(key, group, src, dst, device).start()

    def arrive(self, key, group, ref):
        self.make(key, group, ref, ref, self.other).wait_recv()

    def left(self, key, group, ref):
        self.make(key, group, ref, ref, self.other).wait_send()


def slot_ids(routes_ref, counts_ref):
    row = lax.broadcasted_iota(jnp.int32, (32, 128), 0)
    ids = jnp.full((32, 128), -1, jnp.int32)
    for k in range(CAP):
        ids = jnp.where(row == k, routes_ref[0, k], ids)
    return jnp.where(row < counts_ref[0], ids, -1)


def one_hot(ids):
    lane = lax.broadcasted_iota(jnp.int32, (32, 128), 1)
    return jnp.where(ids == lane, 1.0, 0.0).astype(BF16)


class Place:
    def __init__(self):
        self.c, self.t = lax.axis_index("context"), lax.axis_index("tensor")
        self.z, self.x = lax.div(self.c, NX), lax.rem(self.c, NX)
        self.y, self.core = lax.div(self.t, 2), lax.rem(self.t, 2)
        self.odd = lax.rem(self.x, 2)
        self.pair = lax.div(self.x, 2)

    def at_z(self, dz):
        return lax.rem(self.z + dz + NZ, NZ)

    def at(self, dz, dx):
        return self.at_z(dz) * NX + lax.rem(self.x + dx + NX, NX)

    def dev(self, dz, dx):
        return (self.at(dz, dx), self.t)

    def mate(self, q):
        if q == 1:
            return self.x + 1 - 2 * self.odd
        return lax.rem(self.x + 2, NX) if q == 2 else 3 - self.x

    def mate_at(self, q):
        return self.z * NX + self.mate(q)

    def mate_dev(self, q):
        return (self.mate_at(q), self.t)

    def pair_at(self, dz, other):
        p = 1 - self.pair if other else self.pair
        return pl.ds(self.at_z(dz) * NX + 2 * p, 2)

    def chunk(self, dy, flip=0):
        k = 1 - self.core if flip else self.core
        return lax.rem(self.y + dy + NY, NY) * 2 + k

    def peer(self, dy, flip=0):
        return (self.c, self.chunk(dy, flip))


def flat(v):
    return jnp.concatenate([v[i:i + 1] for i in range(v.shape[0])], axis=1)


PEERS = [(dy, f) for dy in range(NY) for f in (0, 1) if (dy, f) != (0, 0)]


class Paths:
    def __init__(self, tag, net, me, wa):
        self.tag, self.net, self.me = tag, net, me
        self.wa, self.wb = wa, WIDE - wa

    def halves(self, odd):
        cut = 128 if odd else self.wb - 128
        return (0, cut), (cut, self.wb - cut)

    def send(self, key, src, dst, device):
        self.net.send((self.tag,) + key, (self.tag, key[0][0]), src, dst, device)

    def arrive(self, key, ref):
        self.net.arrive((self.tag,) + key, (self.tag, key[0][0]), ref)

    def left(self, ref):
        for part, key, lo, n in (("a", ("a", 2, 0), 0, self.wa), ("b", ("br", 2), self.wa, self.wb)):
            self.net.left((self.tag,) + key, (self.tag, part),
                          ref.at[pl.ds(0, SHARDS - 1), :, pl.ds(lo, n)])

    def longer(self, right, other):
        return right != bool(other)


class Gather(Paths):
    def __init__(self, tag, net, me, wa, g):
        super().__init__(tag, net, me, wa)
        self.g = g

    def part(self, dz, dx, span=None):
        lo, n = span or (0, self.wb)
        return self.g.at[self.me.at(dz, dx), :, pl.ds(self.wa + lo, n)]

    def duo(self, dz, other):
        return self.g.at[self.me.pair_at(dz, other), :, pl.ds(0, self.wa)]

    def pass_on(self, key, ref, device):
        self.send(key, ref, ref, device)

    def a_pass(self, s, other):
        for right, back in ((True, -1), (False, 1)):
            if s < 4 or self.longer(right, other):
                self.pass_on(("a", s, other, right), self.duo(back * (s - 1), other),
                             self.me.dev(-back, 0))

    def a_take(self, s, other):
        for right, back in ((True, -1), (False, 1)):
            if s < 4 or self.longer(right, other):
                self.arrive(("a", s, other, right), self.duo(back * s, other))

    def b_pass(self, s):
        r, l = self.halves(0) if s == 4 else (None, None)
        self.pass_on(("br", s), self.part(1 - s, 0, r), self.me.dev(1, 0))
        self.pass_on(("bl", s), self.part(s - 1, 0, l), self.me.dev(-1, 0))

    def b_take(self, s):
        r, l = self.halves(0) if s == 4 else (None, None)
        self.arrive(("br", s), self.part(-s, 0, r))
        self.arrive(("bl", s), self.part(s, 0, l))

    def b_side(self, o):
        r = self.part(o, 0)
        self.pass_on(("bxr", o), r, self.me.dev(0, 1))
        self.pass_on(("bxl", o), r, self.me.dev(0, -1))

    def b_cross(self, o):
        r, l = self.halves(o % 2)
        self.arrive(("bxr", o), self.part(o, -1))
        self.pass_on(("bd",), self.part(o, -1, r), self.me.dev(0, 1))
        self.arrive(("bxl", o), self.part(o, 1))
        self.pass_on(("bd",), self.part(o, 1, l), self.me.dev(0, -1))

    def start(self):
        own = self.g.at[self.me.c, :, pl.ds(0, self.wa)]
        self.b_pass(1)
        for q in (1, 2, 3):
            self.pass_on(("ax", q), own, self.me.mate_dev(q))
        self.b_side(0)

    def begin_ring(self):
        for q in (1, 2, 3):
            self.arrive(("ax", q), self.g.at[self.me.mate_at(q), :, pl.ds(0, self.wa)])
            if q != 2:
                self.a_pass(1, int(q == 3))

    def step(self, s):
        self.b_take(s)
        if s < 4:
            self.b_pass(s + 1)
            self.b_side(-s)
            self.b_side(s)
        else:
            self.b_side(4)
        for other in (0, 1):
            self.a_take(s, other)
            if s < 4:
                self.a_pass(s + 1, other)
        for o in ((0,) if s == 1 else (1 - s, s - 1)):
            self.b_cross(o)

    def drain(self):
        self.b_cross(4)
        self.arrive(("bd",), self.g.at[pl.ds(0, NZ), :, pl.ds(self.wa, self.wb)])


class Scatter(Paths):
    ORDER = (4, 3, -3, 2, -2, 1, -1, 0)

    def __init__(self, tag, net, me, wa, v, za, zb, xa, xb, fin, w):
        super().__init__(tag, net, me, wa)
        self.v = v
        self.za, self.zb, self.xa, self.xb, self.fin, self.w = za, zb, xa, xb, fin, w

    def mine(self, dz, dx):
        return self.v[self.me.at(dz, dx), :, pl.ds(self.wa, self.wb)].astype(F32)

    def duo(self, dz, other):
        return self.v.at[self.me.pair_at(dz, other), :, pl.ds(0, self.wa)]

    def b_start(self, i):
        o = self.ORDER[i]
        k = self.me.at(o, 2)
        for d, (lo, n) in enumerate(self.halves(o % 2)):
            self.send(("bx1", i, d), self.v.at[k, :, pl.ds(self.wa + lo, n)],
                      self.xb.at[i, d, :, pl.ds(lo, n)], self.me.dev(0, 1 - 2 * d))

    def join(self, ref, term, came, rest):
        (lo, n), (at, m) = came, rest
        cols = pl.ds(lo, n)
        ref[:, cols] = (ref[:, cols].astype(F32) + term[:, lo:lo + n]).astype(BF16)
        ref[:, pl.ds(at, m)] = term[:, at:at + m].astype(BF16)

    def b_next(self, i):
        o = self.ORDER[i]
        spans = self.halves(o % 2)
        for d in range(2):
            lo, n = spans[d]
            self.arrive(("bx1", i, d), self.xb.at[i, d, :, pl.ds(lo, n)])
            self.join(self.xb.at[i, d], self.mine(o, 1 - 2 * d), spans[d], spans[1 - d])
            self.send(("bx2", i, d), self.xb.at[i, d], self.xb.at[i, 2 + d], self.me.dev(0, 1 - 2 * d))

    def b_sum(self, i):
        for d in range(2):
            self.arrive(("bx2", i, d), self.xb.at[i, 2 + d])
        return (self.mine(self.ORDER[i], 0)
                + self.xb[i, 2].astype(F32) + self.xb[i, 3].astype(F32))

    def a_ring(self, s):
        for other in (1, 0):
            for d, right in ((0, True), (1, False)):
                ahead = (1 - 2 * d) * (5 - s)
                first = 1 if self.longer(right, other) else 2
                if s < first:
                    continue
                term = self.duo(ahead, other)
                src = term
                if s > first:
                    src = self.za.at[other, d, s - 2]
                    self.arrive(("a", s - 1, other, d), src)
                    src[...] = (src[...].astype(F32) + term[...].astype(F32)).astype(BF16)
                self.send(("a", s, other, d), src, self.za.at[other, d, s - 1],
                          self.me.dev(1 - 2 * d, 0))

    def a_sum(self, other):
        for d in range(2):
            self.arrive(("a", 4, other, d), self.za.at[other, d, 3])
        return (self.duo(0, other)[...].astype(F32)
                + self.za[other, 0, 3].astype(F32) + self.za[other, 1, 3].astype(F32))

    def b_ring(self, s, right=None, left=None):
        spans = self.halves(0)
        for d, (name, term) in enumerate((("br", right), ("bl", left))):
            lo, n = spans[d]
            if s == 1:
                src, dst = self.w.at[:, pl.ds(lo, n)], self.zb.at[d, 0, :, pl.ds(lo, n)]
            else:
                src, dst = self.zb.at[d, s - 2], self.zb.at[d, s - 1]
                if s == 2:
                    self.arrive((name, 1), self.zb.at[d, 0, :, pl.ds(lo, n)])
                    self.join(src, term, spans[d], spans[1 - d])
                else:
                    self.arrive((name, s - 1), src)
                    src[...] = (src[...].astype(F32) + term).astype(BF16)
            self.send((name, s), src, dst, self.me.dev(1 - 2 * d, 0))

    def start(self):
        for i in range(4):
            self.b_start(i)
        self.a_ring(1)
        for i in range(4, 8):
            self.b_start(i)

    def turn(self):
        for i in range(3):
            self.b_next(i)
        self.a_ring(2)
        for i in range(3, 8):
            self.b_next(i)

    def second(self):
        self.w[...] = self.b_sum(0).astype(BF16)
        self.b_ring(1)
        self.a_ring(3)
        self.b_ring(2, self.b_sum(1), self.b_sum(2))

    def third(self):
        self.a_ring(4)
        self.b_ring(3, self.b_sum(3), self.b_sum(4))

    def fourth(self):
        me, odd = self.me, self.me.odd
        for other in (1, 0):
            self.fin[other] = self.a_sum(other).astype(BF16)
        for q, other, k in ((3, 1, 1 - odd), (2, 1, odd), (1, 0, 1 - odd)):
            self.send(("ax",), self.fin.at[other, k], self.xa.at[q], me.mate_dev(q))
        self.b_ring(4, self.b_sum(5), self.b_sum(6))

    def last(self):
        self.arrive(("ax",), self.xa.at[pl.ds(1, 3)])
        a = self.fin[0, self.me.odd].astype(F32)
        for q in (1, 3, 2):
            a = a + self.xa[q].astype(F32)
        for d, name in enumerate(("br", "bl")):
            self.arrive((name, 4), self.zb.at[d, 3])
        b = self.b_sum(7) + self.zb[0, 3].astype(F32) + self.zb[1, 3].astype(F32)
        return jnp.concatenate([a, b], axis=1)


class Unit:
    def __init__(self, net, me, y, h, r1, acc, rd, rf):
        self.net, self.me, self.y, self.h = net, me, y, h
        self.r1, self.acc, self.rd, self.rf = r1, acc, rd, rf

    def pair(self, k, dy):
        return self.y[k, self.me.chunk(dy)].astype(F32) + self.r1[k, dy].astype(F32)

    def share(self, k):
        for dy in (2, 1, 3, 0):
            key = ("c", k, dy) if dy else ("end",)
            self.net.send(key, "u1", self.y.at[k, self.me.chunk(dy, 1)], self.r1.at[k, dy],
                          self.me.peer(0, 1))

    def far(self, k):
        self.net.arrive(("c", k, 2), "u1", self.r1.at[k, 2])
        self.acc[k, 2] = self.pair(k, 2).astype(BF16)
        for i in range(2):
            self.net.send(("d", k, i), "u1", self.acc.at[k, 2, pl.ds(32 * i, 32)],
                          self.rd.at[k, i], self.me.peer(1 - 2 * i))

    def near(self, k):
        for dy, i in ((1, 0), (3, 1)):
            self.net.arrive(("c", k, dy), "u1", self.r1.at[k, dy])
            v = self.pair(k, dy)
            self.net.arrive(("d", k, i), "u1", self.rd.at[k, i])
            lo = 32 * i
            hi = 32 - lo
            self.acc[k, dy, pl.ds(lo, 32)] = (
                v[lo:lo + 32] + self.rd[k, i].astype(F32)
            ).astype(BF16)
            self.acc[k, dy, pl.ds(hi, 32)] = v[hi:hi + 32].astype(BF16)
            self.net.send(("end",), "u1", self.acc.at[k, dy], self.rf.at[k, i],
                          self.me.peer(1 - 2 * i))

    def settle(self):
        self.net.arrive(("end",), "u1", self.y.at[:, pl.ds(0, 3)])
        self.net.left(("end",), "u1", self.y.at[:, pl.ds(0, 7)])

    def total(self, k, rows):
        return (
            self.y[k, self.me.t, rows].astype(F32)
            + self.r1[k, 0, rows].astype(F32)
            + self.rf[k, 0, rows].astype(F32)
            + self.rf[k, 1, rows].astype(F32)
        )

    def spread(self, k):
        own = self.h.at[k, self.me.t]
        self.net.send(("gr", k), "u2", own, own, self.me.peer(1))
        self.net.send(("gl", k), "u2", own, own, self.me.peer(-1))
        self.net.send(("g", k), "u2", own, own, self.me.peer(0, 1))

    def relay(self, k):
        me = self.me
        for key, dy, lo in (("gr", -1, 0), ("gl", 1, 32)):
            ref = self.h.at[k, me.chunk(dy)]
            self.net.arrive((key, k), "u2", ref)
            half = self.h.at[k, me.chunk(dy), pl.ds(lo, 32)]
            self.net.send(("e", k), "u2", half, half, me.peer(-dy))
            self.net.send(("g", k), "u2", ref, ref, me.peer(0, 1))

    def close(self, k):
        me = self.me
        ref = self.h.at[k, me.chunk(2)]
        self.net.arrive(("e", k), "u2", ref)
        self.net.send(("g", k), "u2", ref, ref, me.peer(0, 1))
        self.net.arrive(("g", k), "u2", self.h.at[k, pl.ds(0, 4)])


def block_kernel(
    routes_ref, counts_ref, tok_ref, cot_ref, gain_ref, router_ref, wg_hbm, wu_hbm, wd_hbm,
    mix_ref, gt_ref, gain_out, router_out, gg_hbm, gu_hbm, gd_hbm,
    wg, wu, wd, gx, gs, pad, spot, sel, sel_t, x_all, x_gain, s_all,
    y, h, r1, acc, rd, rf, st_slots, p_slots, prod, vb, vn,
    za_b, zb_b, xa_b, xb_b, fin_b, w_b, za_n, zb_n, xa_n, xb_n, fin_n, w_n,
    cx, cz, sx, sz, go, local_sems, send_sems, recv_sems,
):
    me = Place()
    net = Net(send_sems, recv_sems, me.peer(0, 1))
    barrier = pltpu.get_barrier_semaphore()
    friends = (
        [me.dev(dz, 0) for dz in range(1, NZ)]
        + [me.dev(0, dx) for dx in range(1, NX)]
        + [me.peer(dy, f) for dy, f in PEERS]
    )
    for device in friends:
        pl.semaphore_signal(barrier, inc=1, device_id=device, device_id_type=MESH)
    loads = [
        pltpu.make_async_copy(src, dst, local_sems.at[i])
        for i, (src, dst) in enumerate(((wg_hbm, wg), (wu_hbm, wu), (wd_hbm, wd)))
    ]
    for load in loads:
        load.start()
    hot = one_hot(slot_ids(routes_ref, counts_ref))
    for src, dst in ((tok_ref, gx), (cot_ref, gs)):
        rows = dot(hot, src[...])[:CAP]
        dst[me.c] = jnp.concatenate([rows[:, :WIDE], rows[:, WIDE:]], axis=0).astype(BF16)
    lane8 = lax.broadcasted_iota(jnp.int32, (8, 128), 1)
    cx[0] = jnp.where(lane8 == me.c, counts_ref[0].astype(F32), 0.0)
    pl.semaphore_wait(barrier, len(friends))

    gather_x = Gather("X", net, me, 128, gx)
    gather_s = Gather("S", net, me, 256, gs)
    unit = Unit(net, me, y, h, r1, acc, rd, rf)

    gather_x.start()
    for dx in (1, 2, 3):
        net.send(("cx",), "cx", cx.at[0], cx.at[dx], me.dev(0, dx))
    gather_x.begin_ring()
    net.arrive(("cx",), "cx", cx.at[pl.ds(1, 3)])
    cz[0] = cx[0] + cx[1] + cx[2] + cx[3]
    for dz in range(1, NZ):
        net.send(("cz",), "cz", cz.at[0], cz.at[dz], me.dev(dz, 0))
    gather_x.step(1)
    gather_s.start()
    gather_x.step(2)
    gather_s.begin_ring()
    net.arrive(("cz",), "cz", cz.at[pl.ds(1, NZ - 1)])
    held = cz[0]
    for dz in range(1, NZ):
        held = held + cz[dz]

    def place_of(shard, slot, combine):
        ahead = jnp.where(slot >= CAP * shard + CAP, 1.0, 0.0)
        inside = jnp.where(slot >= CAP * shard, 1.0 - ahead, 0.0)
        ahead, inside = ahead.astype(BF16), inside.astype(BF16)
        count, offset, shards = combine(inside, ahead)
        k = (slot[:1] if slot.shape[1] == SLOTS else slot).astype(F32) - CAP * shards
        return jnp.where(k < count, offset + k, -1.0)

    def as_row(inside, ahead):
        c = held.astype(BF16)
        one = jnp.ones((8, 128), BF16)
        return dot(c, inside)[0:1], dot(c, ahead)[0:1], dot(one, ahead)[0:1]

    line = place_of(
        lax.broadcasted_iota(jnp.int32, (128, SLOTS), 0),
        lax.broadcasted_iota(jnp.int32, (128, SLOTS), 1),
        as_row,
    )
    sel[...] = jnp.where(
        line == lax.broadcasted_iota(jnp.int32, (ROWS, SLOTS), 0).astype(F32), 1.0, 0.0
    ).astype(BF16)
    gather_x.step(3)
    eye = lax.broadcasted_iota(jnp.int32, (128, 128), 0) == lax.broadcasted_iota(
        jnp.int32, (128, 128), 1
    )

    def as_column(inside, ahead):
        c = jnp.sum(jnp.where(eye, held[0:1], 0.0), axis=1, keepdims=True)
        c = jnp.broadcast_to(c, (128, 128)).astype(BF16)
        one = jnp.ones((128, 128), BF16)
        return dot(inside, c), dot(ahead, c), dot(ahead, one)

    spot[...] = place_of(
        lax.broadcasted_iota(jnp.int32, (SLOTS, 128), 1),
        lax.broadcasted_iota(jnp.int32, (SLOTS, 128), 0),
        as_column,
    )
    sel_t[...] = jnp.where(
        jnp.concatenate([spot[...]] * 4, axis=1)
        == lax.broadcasted_iota(jnp.int32, (SLOTS, ROWS), 1).astype(F32), 1.0, 0.0
    ).astype(BF16)
    gather_x.step(4)
    gather_s.step(1)
    gather_x.drain()

    def flatten(g):
        @pl.loop(0, NZ)
        def _(i):
            v = g[pl.ds(NX * i, NX)].astype(F32)
            rows = pl.ds(pl.multiple_of(i * (NX * CAP), 32), NX * CAP)
            pad[rows, pl.ds(0, WIDE)] = v[:, :CAP].reshape(NX * CAP, WIDE).astype(BF16)
            pad[rows, pl.ds(WIDE, WIDE)] = v[:, CAP:].reshape(NX * CAP, WIDE).astype(BF16)

    flatten(gx)
    for lo, n in COL_TILES:
        cols = pl.ds(lo, n)
        v = dot(sel[...], pad[:, cols])
        x_all[:, cols] = v.astype(BF16)
        x_gain[:, cols] = (v * gain_ref[:, cols]).astype(BF16)
    loads[0].wait()
    for lo, n in FF_TILES:
        v = dot(x_gain[...], wg[:, pl.ds(lo, n)])
        y[0, :, :, pl.ds(lo, n)] = v.astype(BF16).reshape(8, CHUNK, n)
    unit.share(0)
    gather_s.step(2)
    loads[1].wait()
    for lo, n in FF_TILES:
        v = dot(x_gain[...], wu[:, pl.ds(lo, n)])
        y[1, :, :, pl.ds(lo, n)] = v.astype(BF16).reshape(8, CHUNK, n)
    unit.share(1)
    unit.far(0)
    gather_s.step(3)
    unit.far(1)
    unit.near(0)
    router = flat(router_ref[...].astype(F32))
    sq = jnp.zeros((ROWS, 128), F32)
    lg = jnp.zeros((ROWS, 128), F32)
    for lo in range(0, COLS, 128):
        v = x_all[:, pl.ds(lo, 128)].astype(F32)
        sq = sq + v * v
        lg = lg + v * router[:, lo:lo + 128]
    sq = jnp.sum(sq, axis=1, keepdims=True)
    lg = jnp.sum(lg, axis=1, keepdims=True)
    for i in range(8):
        v = (sq, lg)[i // 4][128 * (i % 4):128 * (i % 4) + 128]
        st_slots[me.t, pl.ds(i, 1)] = jnp.sum(jnp.where(eye, v, 0.0), axis=0, keepdims=True)
    for dy, f in PEERS:
        ref = st_slots.at[me.t]
        net.send(("st",), "st", ref, ref, me.peer(dy, f))
    gather_s.step(4)
    unit.near(1)
    gather_s.drain()
    flatten(gs)
    for lo, n in COL_TILES:
        cols = pl.ds(lo, n)
        s_all[:, cols] = dot(sel[...], pad[:, cols]).astype(BF16)
    loads[2].wait()
    for lo, n in FF_TILES:
        v = contract_cols(s_all[...], wd[pl.ds(lo, n), :])
        y[2, :, :, pl.ds(lo, n)] = v.astype(BF16).reshape(8, CHUNK, n)
    unit.share(2)
    unit.far(2)

    net.arrive(("st",), "st", st_slots.at[pl.ds(0, 7)])
    stat = st_slots[0]
    for k in range(1, 8):
        stat = stat + st_slots[k]
    sub = lax.broadcasted_iota(jnp.int32, (8, 128), 0)
    lane = lax.broadcasted_iota(jnp.int32, (CHUNK, 128), 1)
    row = lax.broadcasted_iota(jnp.int32, (CHUNK, 128), 0)
    at_own = lane == row + me.core * CHUNK

    def column(which):
        line = jnp.sum(jnp.where(sub == which, stat, 0.0), axis=0, keepdims=True)
        return jnp.sum(jnp.where(at_own, line, 0.0), axis=1, keepdims=True)

    inv_rms = lax.rsqrt(column(me.y) / D + EPS)
    weight = jax.nn.sigmoid(column(4 + me.y))
    unit.near(2)
    unit.settle()
    firsts, seconds = [], []
    for i in range(4):
        rows = pl.ds(16 * i, 16)
        inv = inv_rms[16 * i:16 * i + 16]
        w = weight[16 * i:16 * i + 16]
        g_raw, u_raw, d_raw = unit.total(0, rows), unit.total(1, rows), unit.total(2, rows)
        gate, upward = g_raw * inv, u_raw * inv
        sigma = jax.nn.sigmoid(gate)
        act = gate * sigma
        hidden = (act * upward * w).astype(BF16)
        d_hidden = d_raw * (w * inv)
        d_gate = (d_hidden * upward * sigma * (1.0 + gate * (1.0 - sigma))).astype(BF16)
        d_up = (d_hidden * act).astype(BF16)
        h[0, me.t, rows] = hidden
        h[1, me.t, rows] = d_gate
        h[2, me.t, rows] = d_up
        firsts.append(jnp.sum(d_raw * hidden.astype(F32), axis=1, keepdims=True))
        seconds.append(
            jnp.sum(d_gate.astype(F32) * g_raw + d_up.astype(F32) * u_raw, axis=1, keepdims=True)
        )
    for k in range(3):
        unit.spread(k)

    def line_of(parts):
        return jnp.sum(jnp.where(at_own, jnp.concatenate(parts, axis=0), 0.0), axis=0, keepdims=True)

    p_slots[me.t] = jnp.where(sub == me.y, line_of(firsts), 0.0) + jnp.where(
        sub == 4 + me.y, line_of(seconds), 0.0
    )
    for dy, f in PEERS:
        ref = p_slots.at[me.t]
        net.send(("p",), "p", ref, ref, me.peer(dy, f))

    scatter_b = Scatter("B", net, me, 256, vb, za_b, zb_b, xa_b, xb_b, fin_b, w_b)
    scatter_n = Scatter("N", net, me, 128, vn, za_n, zb_n, xa_n, xb_n, fin_n, w_n)

    def all_rows(k):
        return h[k].reshape(ROWS, FFL)

    def expand(v):
        for g in range(2):
            s = sel_t[pl.ds(384 * g, 384), :]
            parts = [
                dot(s, prod[:, pl.ds(WIDE * i, WIDE)]).reshape(16, CAP, WIDE) for i in range(2)
            ]
            v[pl.ds(16 * g, 16)] = jnp.concatenate(parts, axis=1).astype(BF16)

    unit.relay(0)
    unit.close(0)
    for lo, n in COL_TILES:
        cols = pl.ds(lo, n)
        prod[:, cols] = dot(all_rows(0), wd[:, cols]).astype(BF16)
    unit.relay(1)
    expand(vb)
    scatter_b.start()
    unit.relay(2)
    unit.close(1)
    scatter_b.turn()
    unit.close(2)
    for i, (lo, n) in enumerate(COL_TILES):
        cols = pl.ds(lo, n)
        v = contract_cols(all_rows(1), wg[cols, :]) + contract_cols(all_rows(2), wu[cols, :])
        prod[:, cols] = v.astype(BF16)
        line = jnp.sum(v * x_all[:, cols].astype(F32), axis=0, keepdims=True)
        sx[0, pl.ds(8 + 2 * i, 1)] = line[:, :128]
        sx[0, pl.ds(9 + 2 * i, 1)] = line[:, 128:]
    net.arrive(("p",), "p", p_slots.at[pl.ds(0, 7)])
    p = p_slots[0]
    for k in range(1, 8):
        p = p + p_slots[k]
    sx[0, pl.ds(0, 8)] = p
    for dx in (1, 2, 3):
        net.send(("sx",), "sx", sx.at[0], sx.at[dx], me.dev(0, dx))
    scatter_b.second()
    expand(vn)
    scatter_n.start()
    scatter_b.third()
    net.arrive(("sx",), "sx", sx.at[pl.ds(1, 3)])
    sz[0] = sx[0] + sx[1] + sx[2] + sx[3]
    for dz in range(1, NZ):
        net.send(("sz",), "sz", sz.at[0], sz.at[dz], me.dev(dz, 0))

    scatter_n.turn()
    scatter_b.fourth()
    stores = []

    def write(i, src, out):
        store = pltpu.make_async_copy(src, out, local_sems.at[3 + i])
        store.start()
        stores.append(store)

    for lo in range(0, FFL, 128):
        left = h[0, :, :, pl.ds(lo, 128)].reshape(ROWS, 128)
        go[0, pl.ds(lo, 128), :] = contract_rows(left, s_all[...]).astype(BF16)
    write(0, go.at[0, pl.ds(0, FFL)], gd_hbm)
    scatter_n.second()
    for lo in range(0, COLS, 256):
        left = x_gain[:, pl.ds(lo, 256)]
        go[1, pl.ds(lo, 256), pl.ds(0, FFL)] = contract_rows(left, all_rows(1)).astype(BF16)
    write(1, go.at[1, :, pl.ds(0, FFL)], gg_hbm)
    scatter_n.third()
    for lo in range(0, COLS, 256):
        left = x_gain[:, pl.ds(lo, 256)]
        go[2, pl.ds(lo, 256), pl.ds(0, FFL)] = contract_rows(left, all_rows(2)).astype(BF16)
    write(2, go.at[2, :, pl.ds(0, FFL)], gu_hbm)
    branch = scatter_b.last()
    scatter_n.fourth()

    net.arrive(("sz",), "sz", sz.at[pl.ds(1, NZ - 1)])
    tot = sz[0]
    for dz in range(1, NZ):
        tot = tot + sz[dz]
    d_logit = tot[0:4] * (1.0 - jax.nn.sigmoid(stat[4:8]))
    mean_term = tot[4:8] / D / (stat[0:4] / D + EPS)

    d_logit, mean_term = flat(d_logit), flat(mean_term)
    first = d_logit.astype(BF16)
    rest = d_logit - first.astype(F32)
    second = rest.astype(BF16)
    third = (rest - second.astype(F32)).astype(BF16)
    for lo, n in COL_TILES:
        cols = pl.ds(lo, n)
        x = x_all[:, cols]
        line = dot(first, x) + dot(second, x) + dot(third, x)
        for k in range(0, n, 128):
            router_out[pl.ds((lo + k) // 128, 1)] = line[:, k:k + 128]
    gain_out[...] = tot[8:16]
    own = spot[pl.ds(pl.multiple_of(me.c * CAP, 8), CAP), :]
    own = jnp.concatenate([own] * 4, axis=1)
    hit = own == lax.broadcasted_iota(jnp.int32, (CAP, ROWS), 1).astype(F32)
    d_logit = jnp.sum(jnp.where(hit, d_logit, 0.0), axis=1, keepdims=True)
    mean_term = jnp.sum(jnp.where(hit, mean_term, 0.0), axis=1, keepdims=True)

    d_normed = scatter_n.last()
    picked, slope = gx[me.c].astype(F32), gs[me.c].astype(F32)
    mix_ref[...] = picked + branch
    for i in range(2):
        r = slice(CAP * i, CAP * i + CAP)
        feats = slice(WIDE * i, WIDE * i + WIDE)
        gt_ref[pl.ds(CAP * i, CAP), :] = slope[r] + (
            d_normed[r] * gain_ref[:, pl.ds(WIDE * i, WIDE)] - picked[r] * mean_term
            + d_logit * router[:, feats]
        )
    for store in stores:
        store.wait()
    for paths, ref in ((gather_x, gx), (gather_s, gs), (scatter_b, vb), (scatter_n, vn)):
        paths.left(ref)
    net.left(("g", 0), "u2", h.at[:, pl.ds(0, 7)])
    for name, ref, n in (
        ("cx", cx, 3), ("cz", cz, 7), ("sx", sx, 3), ("sz", sz, 7), ("st", st_slots, 7), ("p", p_slots, 7)
    ):
        net.left((name,), name, ref.at[pl.ds(0, n)])


def block(routes, counts, tokens, cotangent, gain, router, w_gate, w_up, w_down):
    vm = pl.BlockSpec(memory_space=VMEM)
    sm = pl.BlockSpec(memory_space=pltpu.SMEM)
    hbm = pl.BlockSpec(memory_space=pl.ANY)
    ring_b, ring_n = (
        [
            VMEM((2, 2, 4, 2, TALL, wa), BF16),
            VMEM((2, 4, TALL, WIDE - wa), BF16),
            VMEM((4, TALL, wa), BF16),
            VMEM((8, 4, TALL, WIDE - wa), BF16),
            VMEM((2, 2, TALL, wa), BF16),
            VMEM((TALL, WIDE - wa), BF16),
        ]
        for wa in (256, 128)
    )
    return pl.pallas_call(
        block_kernel,
        out_shape=(
            jax.ShapeDtypeStruct((TALL, WIDE), F32),
            jax.ShapeDtypeStruct((TALL, WIDE), F32),
            jax.ShapeDtypeStruct((8, 128), F32),
            jax.ShapeDtypeStruct((8, 128), F32),
            jax.ShapeDtypeStruct((COLS, FFL), BF16),
            jax.ShapeDtypeStruct((COLS, FFL), BF16),
            jax.ShapeDtypeStruct((FFL, COLS), BF16),
        ),
        in_specs=[sm] * 2 + [vm] * 4 + [hbm] * 3,
        out_specs=(vm,) * 4 + (hbm,) * 3,
        scratch_shapes=[
            VMEM((COLS, FFL), BF16),
            VMEM((COLS, FFL), BF16),
            VMEM((FFL, COLS), BF16),
            VMEM((SHARDS, TALL, WIDE), BF16),
            VMEM((SHARDS, TALL, WIDE), BF16),
            VMEM((SLOTS, COLS), BF16),
            VMEM((SLOTS, 128), F32),
            VMEM((ROWS, SLOTS), BF16),
            VMEM((SLOTS, ROWS), BF16),
            VMEM((ROWS, COLS), BF16),
            VMEM((ROWS, COLS), BF16),
            VMEM((ROWS, COLS), BF16),
            VMEM((3, 8, CHUNK, FFL), BF16),
            VMEM((3, 8, CHUNK, FFL), BF16),
            VMEM((3, 4, CHUNK, FFL), BF16),
            VMEM((3, 4, CHUNK, FFL), BF16),
            VMEM((3, 2, CHUNK // 2, FFL), BF16),
            VMEM((3, 2, CHUNK, FFL), BF16),
            VMEM((8, 8, 128), F32),
            VMEM((8, 8, 128), F32),
            VMEM((ROWS, COLS), BF16),
            VMEM((SHARDS, TALL, WIDE), BF16),
            VMEM((SHARDS, TALL, WIDE), BF16),
            *ring_b,
            *ring_n,
            VMEM((4, 8, 128), F32),
            VMEM((8, 8, 128), F32),
            VMEM((4, 16, 128), F32),
            VMEM((8, 16, 128), F32),
            VMEM((3, COLS, COLS), BF16),
            pltpu.SemaphoreType.DMA((6,)),
            pltpu.SemaphoreType.DMA((SEND_SEMS,)),
            pltpu.SemaphoreType.DMA((RECV_SEMS,)),
        ],
        compiler_params=pltpu.CompilerParams(
            collective_id=0, has_side_effects=True, vmem_limit_bytes=56 << 20
        ),
        name="block",
    )(routes, counts, tokens, cotangent, gain, router, w_gate, w_up, w_down)


def merge_kernel(
    routes_ref, counts_ref, tok_ref, cot_ref, mix_ref, gt_ref, gain_ref, router_ref, a_hbm, b_hbm, c_hbm,
    mixed_ref, grad_ref, gain_out, router_out, a_out, b_out, c_out,
    a, b, c, sems,
):
    n = 2
    ways = []
    for i, (src, held, dst) in enumerate(((a_hbm, a, a_out), (b_hbm, b, b_out), (c_hbm, c, c_out))):
        rows = src.shape[0] // n
        for j in range(n):
            part = pl.ds(rows * j, rows)
            k = i * n + j
            ways.append((
                pltpu.make_async_copy(src.at[part], held.at[part], sems.at[0, k]),
                pltpu.make_async_copy(held.at[part], dst.at[part], sems.at[1, k]),
            ))
    for come, _ in ways:
        come.start()
    gain_out[...] = gain_ref[...]
    router_out[...] = router_ref[...]
    hot = one_hot(slot_ids(routes_ref, counts_ref))
    picked = contract_rows(hot, jnp.ones((32, 128), BF16))[:, 0:1] > 0.5
    blank = jnp.zeros((32 - CAP, COLS), F32)
    for come, go in ways[:2]:
        come.wait()
        go.start()
    for old, new, out in ((tok_ref, mix_ref, mixed_ref), (cot_ref, gt_ref, grad_ref)):
        rows = jnp.concatenate([new[pl.ds(0, CAP), :], new[pl.ds(CAP, CAP), :]], axis=1)
        rows = jnp.concatenate([rows, blank], axis=0).astype(BF16)
        out[...] = jnp.where(picked, contract_rows(hot, rows), old[...].astype(F32)).astype(BF16)
    for come, go in ways[2:]:
        come.wait()
        go.start()
    for _, go in ways:
        go.wait()


def merge(routes, counts, tokens, cotangent, mixed_rows, grad_rows, gain, router, *grads):
    vm = pl.BlockSpec(memory_space=VMEM)
    sm = pl.BlockSpec(memory_space=pltpu.SMEM)
    hbm = pl.BlockSpec(memory_space=pl.ANY)
    same = [
        jax.ShapeDtypeStruct(v.shape, v.dtype) for v in (tokens, cotangent, gain, router) + grads
    ]
    return pl.pallas_call(
        merge_kernel,
        out_shape=same,
        in_specs=[sm] * 2 + [vm] * 6 + [hbm] * 3,
        out_specs=[vm] * 4 + [hbm] * 3,
        scratch_shapes=[VMEM(v.shape, v.dtype) for v in grads] + [pltpu.SemaphoreType.DMA((2, 6))],
        compiler_params=pltpu.CompilerParams(vmem_limit_bytes=60 << 20),
        name="merge",
    )(routes, counts, tokens, cotangent, mixed_rows, grad_rows, gain, router, *grads)


def body(tokens, norm_gain, router, w_gate, w_up, w_down, routes, counts, cotangent):
    new = block(
        routes, counts, tokens, cotangent, norm_gain[None, :], router.reshape(8, 128),
        w_gate, w_up, w_down,
    )
    mixed, grad_tokens, gain, router, *grads = merge(routes, counts, tokens, cotangent, *new)
    return (mixed, grad_tokens, *grads, gain.reshape(COLS), router.reshape(COLS))


def solution(mesh):
    return jax.shard_map(
        body,
        mesh=mesh,
        in_specs=(
            P("context", "tensor"),
            P("tensor"),
            P("tensor"),
            P("tensor", "context"),
            P("tensor", "context"),
            P("context", "tensor"),
            P("context", None),
            P("context"),
            P("context", "tensor"),
        ),
        out_specs=(
            P("context", "tensor"),
            P("context", "tensor"),
            P("tensor", "context"),
            P("tensor", "context"),
            P("context", "tensor"),
            P("tensor"),
            P("tensor"),
        ),
        check_vma=False,
    )
```

time: 141 us -> 119 us (0.84)
  local copies, waits for them, and re-layouts: 11.4 us -> 0 us
  other arithmetic: 8.31 us -> 0 us
  Pallas kernels: 120 us -> 118 us
    unnamed x16 -> x0, local copies, waits for them, and re-layouts: 8.9 us -> none
    pallas_call x1, Pallas kernels: 120 us -> 111 us  [block(): pl.pallas_call(block_kernel, out_shape=(jax.ShapeDtypeStruct((TALL, WIDE)...]
    pallas_call x0 -> x1, Pallas kernels: none -> 6.65 us  [merge(): pl.pallas_call(merge_kernel, out_shape=same, in_specs=[sm] * 2 + [vm] * 6...]
    scatter x2 -> x0, other arithmetic: 1.91 us -> none  [the longest x1 0.96 us: body(): mixed = tokens.at[local_ids].set(mixed_rows)]
    another operation x2 -> x0, other arithmetic: 1.8 us -> none
where the time goes in v3:
time: 119 us
  Pallas kernels  118 us (99%)
  between operations  1.45 us (1%)
    pallas_call x1, Pallas kernels, block(): pl.pallas_call(block_kernel, out_shape=(jax.ShapeDtypeStruct((TALL, WIDE)...  111 us
    pallas_call x1, Pallas kernels, merge(): pl.pallas_call(merge_kernel, out_shape=same, in_specs=[sm] * 2 + [vm] * 6...  6.65 us

profile of v3, /device:TPU:32, one launch (start us, length us, event | category | flops | bytes accessed | tf_op | source)
XLA Modules:
  0.0 119.0 jit_solution(17507878147436016889)
XLA Ops:
  1.3 110.9 %block.1 = (f32[48,512]{1,0:T(8,128)}, f32[48,512]{1,0:T(8,128)}, f32[8,128]{1,0:T(8,128)}, f32[8,128]{1,0:T(8,128)}, bf16[1024,896]{1,0:T(8,128)(2,1)}, /*index...) custom-call(s32[1,24]{1,0:T(1,128)} %routes_ref.3, s32[1]{0:T(128)S(6)} %copy.16.counts_ref, bf16[128,1024]{1,0:T(8,128)(2,1)} %tok_ref.3, ...), custom_call_target="tpu_custom_call" | custom-call | tf_op jit(solution)/shard_map/block/pallas_call | solution.py:768
  112.2 6.6 %merge.1 = (bf16[128,1024]{1,0:T(8,128)(2,1)}, bf16[128,1024]{1,0:T(8,128)(2,1)}, f32[8,128]{1,0:T(8,128)}, f32[8,128]{1,0:T(8,128)}, bf16[1024,896]{1,0:T(8,128...) custom-call(s32[1,24]{1,0:T(1,128)} %routes_ref.3, s32[1]{0:T(128)S(6)} %copy.16.counts_ref, ...), custom_call_target="tpu_custom_call" | custom-call | tf_op jit(solution)/shard_map/merge/pallas_call | solution.py:867

commit v4 on v3

--- a/solution.py
+++ b/solution.py
@@ -16,7 +16,7 @@
 FFL = 896
 COLS = 1024
 TALL, WIDE = 2 * CAP, COLS // 2
-SEND_SEMS, RECV_SEMS = 16, 232
+SEND_SEMS, RECV_SEMS = 16, 236
 MESH = pl.DeviceIdType.MESH
 VMEM = pltpu.VMEM
 F32 = jnp.float32
@@ -363,7 +363,7 @@
 
     def share(self, k):
         for dy in (2, 1, 3, 0):
-            key = ("c", k, dy) if dy else ("end",)
+            key = ("c", k, dy) if dy else ("end", k)
             self.net.send(key, "u1", self.y.at[k, self.me.chunk(dy, 1)], self.r1.at[k, dy],
                           self.me.peer(0, 1))
 
@@ -385,12 +385,11 @@
                 v[lo:lo + 32] + self.rd[k, i].astype(F32)
             ).astype(BF16)
             self.acc[k, dy, pl.ds(hi, 32)] = v[hi:hi + 32].astype(BF16)
-            self.net.send(("end",), "u1", self.acc.at[k, dy], self.rf.at[k, i],
+            self.net.send(("end", k), "u1", self.acc.at[k, dy], self.rf.at[k, i],
                           self.me.peer(1 - 2 * i))
 
-    def settle(self):
-        self.net.arrive(("end",), "u1", self.y.at[:, pl.ds(0, 3)])
-        self.net.left(("end",), "u1", self.y.at[:, pl.ds(0, 7)])
+    def settle(self, k):
+        self.net.arrive(("end", k), "u1", self.y.at[k, pl.ds(0, 3)])
 
     def total(self, k, rows):
         return (
@@ -427,7 +426,7 @@
     routes_ref, counts_ref, tok_ref, cot_ref, gain_ref, router_ref, wg_hbm, wu_hbm, wd_hbm,
     mix_ref, gt_ref, gain_out, router_out, gg_hbm, gu_hbm, gd_hbm,
     wg, wu, wd, gx, gs, pad, spot, sel, sel_t, x_all, x_gain, s_all,
-    y, h, r1, acc, rd, rf, st_slots, p_slots, prod, vb, vn,
+    y, h, r1, acc, rd, rf, st_slots, p_slots, prod, part, vb, vn,
     za_b, zb_b, xa_b, xb_b, fin_b, w_b, za_n, zb_n, xa_n, xb_n, fin_n, w_n,
     cx, cz, sx, sz, go, local_sems, send_sems, recv_sems,
 ):
@@ -462,15 +461,16 @@
     gather_x.start()
     for dx in (1, 2, 3):
         net.send(("cx",), "cx", cx.at[0], cx.at[dx], me.dev(0, dx))
+    gather_s.start()
     gather_x.begin_ring()
     net.arrive(("cx",), "cx", cx.at[pl.ds(1, 3)])
     cz[0] = cx[0] + cx[1] + cx[2] + cx[3]
     for dz in range(1, NZ):
         net.send(("cz",), "cz", cz.at[0], cz.at[dz], me.dev(dz, 0))
+    gather_s.begin_ring()
     gather_x.step(1)
-    gather_s.start()
+    gather_s.step(1)
     gather_x.step(2)
-    gather_s.begin_ring()
     net.arrive(("cz",), "cz", cz.at[pl.ds(1, NZ - 1)])
     held = cz[0]
     for dz in range(1, NZ):
@@ -497,6 +497,7 @@
     sel[...] = jnp.where(
         line == lax.broadcasted_iota(jnp.int32, (ROWS, SLOTS), 0).astype(F32), 1.0, 0.0
     ).astype(BF16)
+    gather_s.step(2)
     gather_x.step(3)
     eye = lax.broadcasted_iota(jnp.int32, (128, 128), 0) == lax.broadcasted_iota(
         jnp.int32, (128, 128), 1
@@ -517,8 +518,8 @@
         jnp.concatenate([spot[...]] * 4, axis=1)
         == lax.broadcasted_iota(jnp.int32, (SLOTS, ROWS), 1).astype(F32), 1.0, 0.0
     ).astype(BF16)
+    gather_s.step(3)
     gather_x.step(4)
-    gather_s.step(1)
     gather_x.drain()
 
     def flatten(g):
@@ -540,16 +541,26 @@
         v = dot(x_gain[...], wg[:, pl.ds(lo, n)])
         y[0, :, :, pl.ds(lo, n)] = v.astype(BF16).reshape(8, CHUNK, n)
     unit.share(0)
-    gather_s.step(2)
+    gather_s.step(4)
     loads[1].wait()
     for lo, n in FF_TILES:
         v = dot(x_gain[...], wu[:, pl.ds(lo, n)])
         y[1, :, :, pl.ds(lo, n)] = v.astype(BF16).reshape(8, CHUNK, n)
     unit.share(1)
     unit.far(0)
-    gather_s.step(3)
+    gather_s.drain()
+    flatten(gs)
+    for lo, n in COL_TILES:
+        cols = pl.ds(lo, n)
+        s_all[:, cols] = dot(sel[...], pad[:, cols]).astype(BF16)
+    loads[2].wait()
     unit.far(1)
+    for lo, n in FF_TILES:
+        v = contract_cols(s_all[...], wd[pl.ds(lo, n), :])
+        y[2, :, :, pl.ds(lo, n)] = v.astype(BF16).reshape(8, CHUNK, n)
+    unit.share(2)
     unit.near(0)
+
     router = flat(router_ref[...].astype(F32))
     sq = jnp.zeros((ROWS, 128), F32)
     lg = jnp.zeros((ROWS, 128), F32)
@@ -565,18 +576,7 @@
     for dy, f in PEERS:
         ref = st_slots.at[me.t]
         net.send(("st",), "st", ref, ref, me.peer(dy, f))
-    gather_s.step(4)
     unit.near(1)
-    gather_s.drain()
-    flatten(gs)
-    for lo, n in COL_TILES:
-        cols = pl.ds(lo, n)
-        s_all[:, cols] = dot(sel[...], pad[:, cols]).astype(BF16)
-    loads[2].wait()
-    for lo, n in FF_TILES:
-        v = contract_cols(s_all[...], wd[pl.ds(lo, n), :])
-        y[2, :, :, pl.ds(lo, n)] = v.astype(BF16).reshape(8, CHUNK, n)
-    unit.share(2)
     unit.far(2)
 
     net.arrive(("st",), "st", st_slots.at[pl.ds(0, 7)])
@@ -594,8 +594,19 @@
 
     inv_rms = lax.rsqrt(column(me.y) / D + EPS)
     weight = jax.nn.sigmoid(column(4 + me.y))
+    unit.settle(0)
+    unit.settle(1)
+    for i in range(4):
+        rows = pl.ds(16 * i, 16)
+        inv = inv_rms[16 * i:16 * i + 16]
+        gate, upward = unit.total(0, rows) * inv, unit.total(1, rows) * inv
+        h[0, me.t, rows] = (
+            gate * jax.nn.sigmoid(gate) * upward * weight[16 * i:16 * i + 16]
+        ).astype(BF16)
+    unit.spread(0)
     unit.near(2)
-    unit.settle()
+    unit.relay(0)
+    unit.settle(2)
     firsts, seconds = [], []
     for i in range(4):
         rows = pl.ds(16 * i, 16)
@@ -604,20 +615,17 @@
         g_raw, u_raw, d_raw = unit.total(0, rows), unit.total(1, rows), unit.total(2, rows)
         gate, upward = g_raw * inv, u_raw * inv
         sigma = jax.nn.sigmoid(gate)
-        act = gate * sigma
-        hidden = (act * upward * w).astype(BF16)
         d_hidden = d_raw * (w * inv)
         d_gate = (d_hidden * upward * sigma * (1.0 + gate * (1.0 - sigma))).astype(BF16)
-        d_up = (d_hidden * act).astype(BF16)
-        h[0, me.t, rows] = hidden
+        d_up = (d_hidden * (gate * sigma)).astype(BF16)
         h[1, me.t, rows] = d_gate
         h[2, me.t, rows] = d_up
-        firsts.append(jnp.sum(d_raw * hidden.astype(F32), axis=1, keepdims=True))
+        firsts.append(jnp.sum(d_raw * h[0, me.t, rows].astype(F32), axis=1, keepdims=True))
         seconds.append(
             jnp.sum(d_gate.astype(F32) * g_raw + d_up.astype(F32) * u_raw, axis=1, keepdims=True)
         )
-    for k in range(3):
-        unit.spread(k)
+    unit.spread(1)
+    unit.spread(2)
 
     def line_of(parts):
         return jnp.sum(jnp.where(at_own, jnp.concatenate(parts, axis=0), 0.0), axis=0, keepdims=True)
@@ -643,21 +651,35 @@
             ]
             v[pl.ds(16 * g, 16)] = jnp.concatenate(parts, axis=1).astype(BF16)
 
-    unit.relay(0)
     unit.close(0)
     for lo, n in COL_TILES:
         cols = pl.ds(lo, n)
         prod[:, cols] = dot(all_rows(0), wd[:, cols]).astype(BF16)
-    unit.relay(1)
     expand(vb)
     scatter_b.start()
+    unit.relay(1)
+    scatter_b.turn()
     unit.relay(2)
+    stores = []
+
+    def write(i, src, out):
+        store = pltpu.make_async_copy(src, out, local_sems.at[3 + i])
+        store.start()
+        stores.append(store)
+
+    for lo in range(0, FFL, 128):
+        left = h[0, :, :, pl.ds(lo, 128)].reshape(ROWS, 128)
+        go[0, pl.ds(lo, 128), :] = contract_rows(left, s_all[...]).astype(BF16)
+    write(0, go.at[0, pl.ds(0, FFL)], gd_hbm)
     unit.close(1)
-    scatter_b.turn()
+    scatter_b.second()
+    for lo, n in COL_TILES:
+        cols = pl.ds(lo, n)
+        part[:, cols] = contract_cols(all_rows(1), wg[cols, :])
     unit.close(2)
     for i, (lo, n) in enumerate(COL_TILES):
         cols = pl.ds(lo, n)
-        v = contract_cols(all_rows(1), wg[cols, :]) + contract_cols(all_rows(2), wu[cols, :])
+        v = part[:, cols] + contract_cols(all_rows(2), wu[cols, :])
         prod[:, cols] = v.astype(BF16)
         line = jnp.sum(v * x_all[:, cols].astype(F32), axis=0, keepdims=True)
         sx[0, pl.ds(8 + 2 * i, 1)] = line[:, :128]
@@ -669,7 +691,6 @@
     sx[0, pl.ds(0, 8)] = p
     for dx in (1, 2, 3):
         net.send(("sx",), "sx", sx.at[0], sx.at[dx], me.dev(0, dx))
-    scatter_b.second()
     expand(vn)
     scatter_n.start()
     scatter_b.third()
@@ -677,30 +698,18 @@
     sz[0] = sx[0] + sx[1] + sx[2] + sx[3]
     for dz in range(1, NZ):
         net.send(("sz",), "sz", sz.at[0], sz.at[dz], me.dev(dz, 0))
-
     scatter_n.turn()
     scatter_b.fourth()
-    stores = []
-
-    def write(i, src, out):
-        store = pltpu.make_async_copy(src, out, local_sems.at[3 + i])
-        store.start()
-        stores.append(store)
-
-    for lo in range(0, FFL, 128):
-        left = h[0, :, :, pl.ds(lo, 128)].reshape(ROWS, 128)
-        go[0, pl.ds(lo, 128), :] = contract_rows(left, s_all[...]).astype(BF16)
-    write(0, go.at[0, pl.ds(0, FFL)], gd_hbm)
-    scatter_n.second()
     for lo in range(0, COLS, 256):
         left = x_gain[:, pl.ds(lo, 256)]
         go[1, pl.ds(lo, 256), pl.ds(0, FFL)] = contract_rows(left, all_rows(1)).astype(BF16)
     write(1, go.at[1, :, pl.ds(0, FFL)], gg_hbm)
-    scatter_n.third()
+    scatter_n.second()
     for lo in range(0, COLS, 256):
         left = x_gain[:, pl.ds(lo, 256)]
         go[2, pl.ds(lo, 256), pl.ds(0, FFL)] = contract_rows(left, all_rows(2)).astype(BF16)
     write(2, go.at[2, :, pl.ds(0, FFL)], gu_hbm)
+    scatter_n.third()
     branch = scatter_b.last()
     scatter_n.fourth()
 
@@ -743,6 +752,7 @@
         store.wait()
     for paths, ref in ((gather_x, gx), (gather_s, gs), (scatter_b, vb), (scatter_n, vn)):
         paths.left(ref)
+    net.left(("end", 0), "u1", y.at[:, pl.ds(0, 7)])
     net.left(("g", 0), "u2", h.at[:, pl.ds(0, 7)])
     for name, ref, n in (
         ("cx", cx, 3), ("cz", cz, 7), ("sx", sx, 3), ("sz", sz, 7), ("st", st_slots, 7), ("p", p_slots, 7)
@@ -800,6 +810,7 @@
             VMEM((8, 8, 128), F32),
             VMEM((8, 8, 128), F32),
             VMEM((ROWS, COLS), BF16),
+            VMEM((ROWS, COLS), F32),
             VMEM((SHARDS, TALL, WIDE), BF16),
             VMEM((SHARDS, TALL, WIDE), BF16),
             *ring_b,

time: 119 us -> 112 us (0.941)
  Pallas kernels: 118 us -> 110 us
    pallas_call x1, Pallas kernels: 111 us -> 103 us  [block(): pl.pallas_call(block_kernel, out_shape=(jax.ShapeDtypeStruct((TALL, WIDE)...]
where the time goes in v4:
time: 112 us; the launch traced here: 111 us
  Pallas kernels  110 us (98%)
  between operations  1.45 us (1%)
    pallas_call x1, Pallas kernels, block(): pl.pallas_call(block_kernel, out_shape=(jax.ShapeDtypeStruct((TALL, WIDE)...  103 us
    pallas_call x1, Pallas kernels, merge(): pl.pallas_call(merge_kernel, out_shape=same, in_specs=[sm] * 2 + [vm] * 6...  6.65 us

profile of v4, /device:TPU:32, one launch (start us, length us, event | category | flops | bytes accessed | tf_op | source)
XLA Modules:
  0.0 111.0 jit_solution(5620356703706264346)
XLA Ops:
  1.3 102.9 %block.1 = (f32[48,512]{1,0:T(8,128)}, f32[48,512]{1,0:T(8,128)}, f32[8,128]{1,0:T(8,128)}, f32[8,128]{1,0:T(8,128)}, bf16[1024,896]{1,0:T(8,128)(2,1)}, /*index...) custom-call(s32[1,24]{1,0:T(1,128)} %routes_ref.3, s32[1]{0:T(128)S(6)} %copy.16.counts_ref, bf16[128,1024]{1,0:T(8,128)(2,1)} %tok_ref.3, ...), custom_call_target="tpu_custom_call" | custom-call | tf_op jit(solution)/shard_map/block/pallas_call | solution.py:778
  104.2 6.6 %merge.1 = (bf16[128,1024]{1,0:T(8,128)(2,1)}, bf16[128,1024]{1,0:T(8,128)(2,1)}, f32[8,128]{1,0:T(8,128)}, f32[8,128]{1,0:T(8,128)}, bf16[1024,896]{1,0:T(8,128...) custom-call(s32[1,24]{1,0:T(1,128)} %routes_ref.3, s32[1]{0:T(128)S(6)} %copy.16.counts_ref, ...), custom_call_target="tpu_custom_call" | custom-call | tf_op jit(solution)/shard_map/merge/pallas_call | solution.py:878

commit v5 on v4

--- a/solution.py
+++ b/solution.py
@@ -226,7 +226,6 @@
             self.b_cross(o)
 
     def drain(self):
-        self.b_cross(4)
         self.arrive(("bd",), self.g.at[pl.ds(0, NZ), :, pl.ds(self.wa, self.wb)])
 
 
@@ -520,7 +519,10 @@
     ).astype(BF16)
     gather_s.step(3)
     gather_x.step(4)
+    gather_s.step(4)
+    gather_x.b_cross(4)
     gather_x.drain()
+    gather_s.b_cross(4)
 
     def flatten(g):
         @pl.loop(0, NZ)
@@ -541,14 +543,13 @@
         v = dot(x_gain[...], wg[:, pl.ds(lo, n)])
         y[0, :, :, pl.ds(lo, n)] = v.astype(BF16).reshape(8, CHUNK, n)
     unit.share(0)
-    gather_s.step(4)
+    gather_s.drain()
     loads[1].wait()
     for lo, n in FF_TILES:
         v = dot(x_gain[...], wu[:, pl.ds(lo, n)])
         y[1, :, :, pl.ds(lo, n)] = v.astype(BF16).reshape(8, CHUNK, n)
     unit.share(1)
     unit.far(0)
-    gather_s.drain()
     flatten(gs)
     for lo, n in COL_TILES:
         cols = pl.ds(lo, n)
@@ -832,58 +833,63 @@
 
 
 def merge_kernel(
-    routes_ref, counts_ref, tok_ref, cot_ref, mix_ref, gt_ref, gain_ref, router_ref, a_hbm, b_hbm, c_hbm,
-    mixed_ref, grad_ref, gain_out, router_out, a_out, b_out, c_out,
-    a, b, c, sems,
+    routes_ref, counts_ref, tok_hbm, cot_hbm, mix_hbm, gt_hbm, gain_hbm, router_hbm, a_hbm, b_hbm, c_hbm,
+    mixed_out, grad_out, gain_out, router_out, a_out, b_out, c_out,
+    tok, cot, mix, gt, gain, router, a, b, c, mixed, grad, in_sems, out_sems,
 ):
-    n = 2
-    ways = []
-    for i, (src, held, dst) in enumerate(((a_hbm, a, a_out), (b_hbm, b, b_out), (c_hbm, c, c_out))):
-        rows = src.shape[0] // n
-        for j in range(n):
+    pieces = [
+        (mix_hbm, mix, None), (gt_hbm, gt, None), (tok_hbm, tok, None), (cot_hbm, cot, None),
+        (gain_hbm, gain, gain_out), (router_hbm, router, router_out),
+    ]
+    for src, held, dst in ((a_hbm, a, a_out), (b_hbm, b, b_out), (c_hbm, c, c_out)):
+        rows = src.shape[0] // 2
+        for j in range(2):
             part = pl.ds(rows * j, rows)
-            k = i * n + j
-            ways.append((
-                pltpu.make_async_copy(src.at[part], held.at[part], sems.at[0, k]),
-                pltpu.make_async_copy(held.at[part], dst.at[part], sems.at[1, k]),
-            ))
-    for come, _ in ways:
-        come.start()
-    gain_out[...] = gain_ref[...]
-    router_out[...] = router_ref[...]
+            pieces.append((src.at[part], held.at[part], dst.at[part]))
+    come = [
+        pltpu.make_async_copy(src, held, in_sems.at[k]) for k, (src, held, _) in enumerate(pieces)
+    ]
+    for copy in come:
+        copy.start()
+    gone = []
+
+    def leave(held, dst):
+        copy = pltpu.make_async_copy(held, dst, out_sems.at[len(gone)])
+        copy.start()
+        gone.append(copy)
+
     hot = one_hot(slot_ids(routes_ref, counts_ref))
     picked = contract_rows(hot, jnp.ones((32, 128), BF16))[:, 0:1] > 0.5
     blank = jnp.zeros((32 - CAP, COLS), F32)
-    for come, go in ways[:2]:
-        come.wait()
-        go.start()
-    for old, new, out in ((tok_ref, mix_ref, mixed_ref), (cot_ref, gt_ref, grad_ref)):
+    for copy in come[:4]:
+        copy.wait()
+    for old, new, held, dst in ((tok, mix, mixed, mixed_out), (cot, gt, grad, grad_out)):
         rows = jnp.concatenate([new[pl.ds(0, CAP), :], new[pl.ds(CAP, CAP), :]], axis=1)
         rows = jnp.concatenate([rows, blank], axis=0).astype(BF16)
-        out[...] = jnp.where(picked, contract_rows(hot, rows), old[...].astype(F32)).astype(BF16)
-    for come, go in ways[2:]:
-        come.wait()
-        go.start()
-    for _, go in ways:
-        go.wait()
-
-
-def merge(routes, counts, tokens, cotangent, mixed_rows, grad_rows, gain, router, *grads):
-    vm = pl.BlockSpec(memory_space=VMEM)
+        held[...] = jnp.where(picked, contract_rows(hot, rows), old[...].astype(F32)).astype(BF16)
+        leave(held, dst)
+    for copy, (_, held, dst) in zip(come[4:], pieces[4:]):
+        copy.wait()
+        leave(held, dst)
+    for copy in gone:
+        copy.wait()
+
+
+def merge(routes, counts, tokens, cotangent, *new):
     sm = pl.BlockSpec(memory_space=pltpu.SMEM)
     hbm = pl.BlockSpec(memory_space=pl.ANY)
-    same = [
-        jax.ShapeDtypeStruct(v.shape, v.dtype) for v in (tokens, cotangent, gain, router) + grads
-    ]
+    out = (tokens, cotangent) + new[2:]
     return pl.pallas_call(
         merge_kernel,
-        out_shape=same,
-        in_specs=[sm] * 2 + [vm] * 6 + [hbm] * 3,
-        out_specs=[vm] * 4 + [hbm] * 3,
-        scratch_shapes=[VMEM(v.shape, v.dtype) for v in grads] + [pltpu.SemaphoreType.DMA((2, 6))],
+        out_shape=[jax.ShapeDtypeStruct(v.shape, v.dtype) for v in out],
+        in_specs=[sm] * 2 + [hbm] * 9,
+        out_specs=[hbm] * 7,
+        scratch_shapes=[VMEM(v.shape, v.dtype) for v in (tokens, cotangent) + new]
+        + [VMEM(v.shape, v.dtype) for v in (tokens, cotangent)]
+        + [pltpu.SemaphoreType.DMA((12,)), pltpu.SemaphoreType.DMA((10,))],
         compiler_params=pltpu.CompilerParams(vmem_limit_bytes=60 << 20),
         name="merge",
-    )(routes, counts, tokens, cotangent, mixed_rows, grad_rows, gain, router, *grads)
+    )(routes, counts, tokens, cotangent, *new)
 
 
 def body(tokens, norm_gain, router, w_gate, w_up, w_down, routes, counts, cotangent):

time: 112 us -> 109 us (0.973)
  Pallas kernels: 110 us -> 106 us
    pallas_call x1, Pallas kernels: 103 us -> 100 us  [block(): pl.pallas_call(block_kernel, out_shape=(jax.ShapeDtypeStruct((TALL, WIDE)...]
where the time goes in v5:
time: 109 us; the launch traced here: 108 us
  Pallas kernels  106 us (97%)
  between operations  1.45 us (1%)
    pallas_call x1, Pallas kernels, block(): pl.pallas_call(block_kernel, out_shape=(jax.ShapeDtypeStruct((TALL, WIDE)...  100 us
    pallas_call x1, Pallas kernels, merge(): pl.pallas_call(merge_kernel, out_shape=[jax.ShapeDtypeStruct(v.shape, v.d...  5.98 us

profile of v5, /device:TPU:32, one launch (start us, length us, event | category | flops | bytes accessed | tf_op | source)
XLA Modules:
  0.0 107.8 jit_solution(2297790664097587081)
XLA Ops:
  1.3 100.4 %block.1 = (f32[48,512]{1,0:T(8,128)}, f32[48,512]{1,0:T(8,128)}, f32[8,128]{1,0:T(8,128)}, f32[8,128]{1,0:T(8,128)}, bf16[1024,896]{1,0:T(8,128)(2,1)}, /*index...) custom-call(s32[1,24]{1,0:T(1,128)} %routes_ref.3, s32[1]{0:T(128)S(6)} %copy.16.counts_ref, bf16[128,1024]{1,0:T(8,128)(2,1)} %tok_hbm.1, ...), custom_call_target="tpu_custom_call" | custom-call | tf_op jit(solution)/shard_map/block/pallas_call | solution.py:779
  101.7 6.0 %merge.1 = (bf16[128,1024]{1,0:T(8,128)(2,1)}, bf16[128,1024]{1,0:T(8,128)(2,1)}, f32[8,128]{1,0:T(8,128)}, f32[8,128]{1,0:T(8,128)}, bf16[1024,896]{1,0:T(8,128...) custom-call(s32[1,24]{1,0:T(1,128)} %routes_ref.3, s32[1]{0:T(128)S(6)} %copy.16.counts_ref, ...), custom_call_target="tpu_custom_call" | custom-call | tf_op jit(solution)/shard_map/merge/pallas_call | solution.py:882

commit v6 on v5

--- a/solution.py
+++ b/solution.py
@@ -659,8 +659,8 @@
     expand(vb)
     scatter_b.start()
     unit.relay(1)
+    unit.relay(2)
     scatter_b.turn()
-    unit.relay(2)
     stores = []
 
     def write(i, src, out):
@@ -668,10 +668,6 @@
         store.start()
         stores.append(store)
 
-    for lo in range(0, FFL, 128):
-        left = h[0, :, :, pl.ds(lo, 128)].reshape(ROWS, 128)
-        go[0, pl.ds(lo, 128), :] = contract_rows(left, s_all[...]).astype(BF16)
-    write(0, go.at[0, pl.ds(0, FFL)], gd_hbm)
     unit.close(1)
     scatter_b.second()
     for lo, n in COL_TILES:
@@ -695,6 +691,10 @@
     expand(vn)
     scatter_n.start()
     scatter_b.third()
+    for lo in range(0, FFL, 128):
+        left = h[0, :, :, pl.ds(lo, 128)].reshape(ROWS, 128)
+        go[0, pl.ds(lo, 128), :] = contract_rows(left, s_all[...]).astype(BF16)
+    write(0, go.at[0, pl.ds(0, FFL)], gd_hbm)
     net.arrive(("sx",), "sx", sx.at[pl.ds(1, 3)])
     sz[0] = sx[0] + sx[1] + sx[2] + sx[3]
     for dz in range(1, NZ):

time: 109 us -> 109 us (level)
  no operation moved by 1% of the time
where the time goes in v6:
time: 109 us; the launch traced here: 108 us
  Pallas kernels  106 us (97%)
  between operations  1.45 us (1%)
    pallas_call x1, Pallas kernels, block(): pl.pallas_call(block_kernel, out_shape=(jax.ShapeDtypeStruct((TALL, WIDE)...  100 us
    pallas_call x1, Pallas kernels, merge(): pl.pallas_call(merge_kernel, out_shape=[jax.ShapeDtypeStruct(v.shape, v.d...  6 us

profile of v6, /device:TPU:32, one launch (start us, length us, event | category | flops | bytes accessed | tf_op | source)
XLA Modules:
  0.0 107.7 jit_solution(1698564557521507176)
XLA Ops:
  1.3 100.3 %block.1 = (f32[48,512]{1,0:T(8,128)}, f32[48,512]{1,0:T(8,128)}, f32[8,128]{1,0:T(8,128)}, f32[8,128]{1,0:T(8,128)}, bf16[1024,896]{1,0:T(8,128)(2,1)}, /*index...) custom-call(s32[1,24]{1,0:T(1,128)} %routes_ref.3, s32[1]{0:T(128)S(6)} %copy.16.counts_ref, bf16[128,1024]{1,0:T(8,128)(2,1)} %tok_hbm.1, ...), custom_call_target="tpu_custom_call" | custom-call | tf_op jit(solution)/shard_map/block/pallas_call | solution.py:779
  101.5 6.0 %merge.1 = (bf16[128,1024]{1,0:T(8,128)(2,1)}, bf16[128,1024]{1,0:T(8,128)(2,1)}, f32[8,128]{1,0:T(8,128)}, f32[8,128]{1,0:T(8,128)}, bf16[1024,896]{1,0:T(8,128...) custom-call(s32[1,24]{1,0:T(1,128)} %routes_ref.3, s32[1]{0:T(128)S(6)} %copy.16.counts_ref, ...), custom_call_target="tpu_custom_call" | custom-call | tf_op jit(solution)/shard_map/merge/pallas_call | solution.py:882
